TPU v7x, 128 devices: a whole 4x4x4 slice. The times are simulated.
128 devices in a mesh: row: 8 (over z, core), col: 16 (over x, y).
Axes of the slice: x: 4, y: 4, z: 4, core: 2. Of those that a mesh axis runs over, the one named last changes fastest.
Arguments:
- coarse: bfloat16 [512, 64, 256], P(('row', 'col')), may hold values from -6 to 6
- noisy: bfloat16 [16, 256, 4096], P(None, 'row', 'col'), may hold values from -6 to 6
- cotangent: bfloat16 [64, 256, 4096], P(None, 'row', 'col'), may hold values from -6 to 6
- interp_rows: bfloat16 [8, 32, 4], replicated, may hold values from -1.5 to 1.5
- interp_cols: bfloat16 [128, 256], replicated, may hold values from -0.5 to 0.5
- first_weight: bfloat16 [3, 3, 64, 80], replicated, may hold values from -0.21875 to 0.21875
- second_weight: bfloat16 [3, 3, 64, 64], replicated, may hold values from -0.25 to 0.25
- block_ids: int32 [128, 4], P(('row', 'col')), may hold values from 0 to 127, as said below
- weight_ids: int32 [128, 4], P(('row', 'col')), may hold values from 0 to 7
- col_start: int32 [16], P('col'), may hold values from 0 to 128
Outputs:
- fine_out: bfloat16 [64, 256, 4096], P(None, 'row', 'col')
- first_grad: float32 [3, 3, 64, 80], replicated
- second_grad: float32 [3, 3, 64, 64], replicated
- coarse_grad: float32 [512, 64, 256], P(('row', 'col'))
Inputs may be any that keep to these rules, and one draw needn't show every extreme that they name: block_ids of a tile in fine-tile row r lie from r * 16 - 2 to (r + 1) * 16 + 1.
All inputs are finite; a program needn't handle non-finite values.
Results may differ from a plain program's by a relative error of at most 0.0075.
Values may be sent and summed in bfloat16 or wider, within the bound.
A program may use at most 192 MiB of HBM per device.

v0:
```python
import jax
import jax.numpy as jnp
from jax import lax
from jax.sharding import PartitionSpec as P

HB = 2
K = 4


def with_halo(cells, sides, width):
    for axis, dim in sides:
        count = lax.axis_size(axis)
        ends = count - 1
        head = lax.slice_in_dim(cells, 0, width, axis=dim)
        tail = lax.slice_in_dim(cells, cells.shape[dim] - width, cells.shape[dim], axis=dim)
        cells = jnp.concatenate(
            [
                lax.ppermute(tail, axis, [(i, (i + 1) % count) for i in range(ends)]),
                cells,
                lax.ppermute(head, axis, [((i + 1) % count, i) for i in range(ends)]),
            ],
            axis=dim,
        )
    return cells


def from_behind(block, axis, distance):
    devices = range(lax.axis_size(axis))
    route = [(i - distance, i) for i in devices if i - distance in devices]
    return lax.ppermute(block, axis, route)


def shifted(padded, row_off, col_off, tile_rows, tile_cols):
    return padded[:, row_off : row_off + tile_rows, col_off : col_off + tile_cols].reshape(
        padded.shape[0], tile_rows * tile_cols
    )


def conv_apply(weights, padded, tile_rows, tile_cols):
    summed = None
    for row_off in range(3):
        for col_off in range(3):
            product = jnp.dot(
                weights[row_off, col_off],
                shifted(padded, row_off, col_off, tile_rows, tile_cols),
                preferred_element_type=jnp.float32,
            )
            summed = product if summed is None else summed + product
    return summed.reshape(weights.shape[2], tile_rows, tile_cols)


def conv_adjoint(weights, padded, tile_rows, tile_cols):
    summed = None
    for row_off in range(3):
        for col_off in range(3):
            product = lax.dot_general(
                weights[row_off, col_off],
                shifted(padded, 2 - row_off, 2 - col_off, tile_rows, tile_cols),
                (((0,), (0,)), ((), ())),
                preferred_element_type=jnp.float32,
            )
            summed = product if summed is None else summed + product
    return summed.reshape(weights.shape[3], tile_rows, tile_cols)


def weight_grad(gradient, padded, tile_rows, tile_cols):
    flat = gradient.reshape(gradient.shape[0], tile_rows * tile_cols)
    rows_out = []
    for row_off in range(3):
        rows_out.append(
            jnp.stack(
                [
                    lax.dot_general(
                        flat,
                        shifted(padded, row_off, col_off, tile_rows, tile_cols),
                        (((1,), (1,)), ((), ())),
                        preferred_element_type=jnp.float32,
                    )
                    for col_off in range(3)
                ]
            )
        )
    return jnp.stack(rows_out)


def silu_slope(active):
    sigma = jax.nn.sigmoid(active)
    return sigma * (1.0 + active * (1.0 - sigma))


def local(
    coarse,
    noisy,
    cotangent,
    interp_rows,
    interp_cols,
    first_weight,
    second_weight,
    block_ids,
    weight_ids,
    col_start,
):
    col_count = lax.axis_size("col")
    row_index = lax.axis_index("row")
    tile_rows, tile_cols = (noisy.shape[1], noisy.shape[2])
    block_rows = coarse.shape[0]
    channels = coarse.shape[1]
    window = interp_cols.shape[0]
    gathered = lax.all_gather(coarse, "col", axis=0, tiled=True)
    nearby = lax.dynamic_slice_in_dim(gathered, col_start[0], window, 2)
    rim_rows = HB * block_rows
    extended = with_halo(nearby, (("row", 0),), rim_rows)
    first_block = row_index * col_count - HB
    local_rows = (block_ids[0] - first_block) * block_rows
    blocks = jnp.stack(
        [lax.dynamic_slice_in_dim(extended, local_rows[slot], block_rows, 0) for slot in range(K)]
    )
    selector = (
        weight_ids[0][:, None] == jnp.arange(interp_rows.shape[0], dtype=jnp.int32)[None, :]
    ).astype(jnp.bfloat16)
    table = jnp.einsum(
        "kn,nfi->kfi", selector, interp_rows, preferred_element_type=jnp.float32
    ).astype(jnp.bfloat16)
    section = jnp.einsum("kfi,kicw->cfw", table, blocks, preferred_element_type=jnp.float32).astype(
        jnp.bfloat16
    )
    cond = jnp.einsum(
        "cfw,wx->cfx", section, interp_cols, preferred_element_type=jnp.float32
    ).astype(jnp.bfloat16)
    inputs = jnp.concatenate([noisy, cond], 0)
    input_pad = with_halo(inputs, (("row", 1), ("col", 2)), 1)
    first_act = conv_apply(first_weight, input_pad, tile_rows, tile_cols)
    hidden = jax.nn.silu(first_act).astype(jnp.bfloat16)
    hidden_pad = with_halo(hidden, (("row", 1), ("col", 2)), 1)
    fine_out = conv_apply(second_weight, hidden_pad, tile_rows, tile_cols).astype(jnp.bfloat16)
    second_local = weight_grad(cotangent, hidden_pad, tile_rows, tile_cols)
    cot_pad = with_halo(cotangent, (("row", 1), ("col", 2)), 1)
    hidden_grad = conv_adjoint(second_weight, cot_pad, tile_rows, tile_cols)
    act_grad = (hidden_grad * silu_slope(first_act)).astype(jnp.bfloat16)
    first_local = weight_grad(act_grad, input_pad, tile_rows, tile_cols)
    first_grad, second_grad = lax.psum((first_local, second_local), ("row", "col"))
    act_pad = with_halo(act_grad, (("row", 1), ("col", 2)), 1)
    noise_channels = noisy.shape[0]
    cond_grad = conv_adjoint(
        first_weight[:, :, :, noise_channels:], act_pad, tile_rows, tile_cols
    ).astype(jnp.bfloat16)
    section_grad = jnp.einsum(
        "cfx,wx->cfw", cond_grad, interp_cols, preferred_element_type=jnp.float32
    ).astype(jnp.bfloat16)
    block_grads = jnp.einsum(
        "kfi,cfw->kicw", table, section_grad, preferred_element_type=jnp.float32
    )
    ext_grad = jnp.zeros(extended.shape, jnp.float32)
    for slot in range(K):
        current = lax.dynamic_slice_in_dim(ext_grad, local_rows[slot], block_rows, 0)
        ext_grad = lax.dynamic_update_slice_in_dim(
            ext_grad, current + block_grads[slot], local_rows[slot], 0
        )
    from_below = from_behind(ext_grad[-rim_rows:].astype(jnp.bfloat16), "row", 1).astype(
        jnp.float32
    )
    from_above = from_behind(ext_grad[:rim_rows].astype(jnp.bfloat16), "row", -1).astype(
        jnp.float32
    )
    band_grad = ext_grad[rim_rows:-rim_rows]
    band_grad = band_grad.at[:rim_rows].add(from_below).at[-rim_rows:].add(from_above)
    spread = jnp.zeros((col_count * block_rows, channels, coarse.shape[2]), jnp.float32)
    spread = lax.dynamic_update_slice_in_dim(spread, band_grad, col_start[0], 2)
    coarse_grad = lax.psum_scatter(spread, "col", scatter_dimension=0, tiled=True)
    return (fine_out, first_grad, second_grad, coarse_grad)


def solution(mesh):
    in_specs = (
        P(("row", "col"), None, None),
        P(None, "row", "col"),
        P(None, "row", "col"),
        P(),
        P(),
        P(),
        P(),
        P(("row", "col"), None),
        P(("row", "col"), None),
        P("col"),
    )
    out_specs = (P(None, "row", "col"), P(), P(), P(("row", "col"), None, None))
    return jax.shard_map(local, mesh=mesh, in_specs=in_specs, out_specs=out_specs, check_vma=False)
```

profile of v0, /device:TPU:1, one launch (start us, length us, event | category | flops | bytes accessed | tf_op | source)
XLA Modules:
  0.0 520.5 jit_solution(15698536943547691420)
XLA Ops:
  7.3 4.7 copy.310
  12.9 3.3 collective-permute-start.11
  16.2 3.5 collective-permute-start.10
  32.4 4.6 collective-permute-start.13
  44.8 4.6 pad_maximum_fusion
  49.4 4.9 fusion.210
  54.3 4.9 copy.320
  59.2 2.8 copy.396
  62.0 4.9 copy.318
  66.9 2.8 copy.394
  69.7 4.9 copy.317
  74.5 2.8 copy.393
  77.4 4.9 copy.313
  82.2 2.9 copy.388
  85.1 5.2 %copy.315 = bf16[64,32,256]{2,1,0:T(8,128)(2,1)} copy(bf16[64,32,256]{0,1,2:T(8,128)(2,1)} %get-tuple-element.127) | data formatting | bytes 2097152 | tf_op jit(solution)/shard_map/slice | solution.py:34
  90.3 2.8 copy.390
  93.2 3.5 copy.316
  112.1 3.6 collective-permute-start
  125.5 4.4 collective-permute-start.2
  129.9 6.3 %fusion.4 = f32[64,8192]{1,0:T(8,128)} fusion(f32[64,8192]{1,0:T(8,128)} %convolution_bitcast_fusion, f32[64,8192]{1,0:T(8,128)} %convolution_bitcast_fusion.1, f32[64,8192]{1,0:T(8,128)} %convolution_bitcast_fusion.2, f32[64,8192]{1,0:T(8,128)} %convolution_bitcast_fusion.3, f32[64,8192]{1,0:T(8,128)} %fusion, bf16[64,8192]{1,0:T(8,128)(2,1)S(1)} %bitcast.508, ...), kind=kOutput, calls=%fused_computation.32 | convolution fusion | flops 69730304 | bytes 13647872 | tf_op jit(solution)/shard_map/dot_general | solution.py:56
  142.1 4.0 collective-permute-start.4
  156.5 6.4 %pad_maximum_fusion.1 = (bf16[80,34,257]{2,1,0:T(8,128)(2,1)S(1)}, bf16[80,34,257]{2,1,0:T(8,128)(2,1)S(1)}) fusion(bf16[80,34,1]{2,1,0:T(8,128)(2,1)S(1)} %copy.295, bf16[80,1,256]{2,1,0:T(2,128)(2,1)S(1)} %collective-permute-done.3, bf16[64,32,256]{2,1,0:T(8,128)(2,1)S(1)} %convolution_convert_fusion, bf16[16,32,256]{2,1,0:T(8,128)(2,1)S(1)} %copy-done.31, ...), kind=kLoop, calls=%fused_computation.42 | loop fusion | flops 13980800 | bytes 4199680 | tf_op jit(solution)/shard_map/concatenate | solution.py:16
  162.9 3.9 fusion.212
  199.8 3.6 collective-permute-start.6
  205.4 3.6 collective-permute-start.14
  216.5 4.6 collective-permute-start.8
  224.4 4.1 collective-permute-start.17
  274.6 2.7 collective-permute-start.18
  285.3 2.8 copy.354
  290.7 16.4 %dynamic_update_slice.19 = f32[64,64,256]{2,1,0:T(8,128)} dynamic-update-slice(f32[64,64,256]{2,1,0:T(8,128)} %broadcast_in_dim.7, f32[64,64,128]{2,1,0:T(8,128)S(1)} %copy.354, s32[]{:T(128)} %constant.69.clone.1, s32[]{:T(128)} %constant.69.clone.1, s32[]{:T(128)S(6)} %select_n.10) | dynamic-update-slice | bytes 4194308 | tf_op jit(solution)/shard_map/dynamic_update_slice | solution.py:168
  320.5 112.7 %all-reduce.3.cloned.1.call-done = (f32[3,3,64,80]{3,2,1,0:T(8,128)}, f32[3,3,64,64]{2,3,1,0:T(8,128)}) async-done(((f32[3,3,64,80]{3,2,1,0:T(8,128)}, f32[3,3,64,64]{2,3,1,0:T(8,128)}), (f32[3,3,64,80]{3,2,1,0:T(8,128)}, f32[3,3,64,64]{2,3,1,0:T(8,128)})) %all-reduce.3.cloned.1.call-update) | async-done | bytes 331792 | tf_op jit(solution)/shard_map/psum | solution.py:141
  435.1 76.7 %reduce-scatter.2.cloned.1.call-done = f32[4,64,256]{2,1,0:T(8,128)} async-done(((f32[64,64,256]{2,1,0:T(8,128)}), f32[4,64,256]{2,1,0:T(8,128)}) %reduce-scatter.2.cloned.1.call-update) | async-done | bytes 262160 | tf_op jit(solution)/shard_map/reduce_scatter | solution.py:169
  (292 shorter events, 172.6 us)
Async XLA Ops:
  7.2 113.9 %copy-start = (bf16[128,256]{1,0:T(8,128)(2,1)S(1)}, bf16[128,256]{1,0:T(8,128)(2,1)}, u32[]{:S(2)}) copy-start(bf16[128,256]{1,0:T(8,128)(2,1)} %param.18) | copy-start | bytes 196612
  7.2 18.6 %copy-start.7 = (bf16[64,32,256]{2,1,0:T(8,128)(2,1)S(1)}, bf16[64,32,256]{2,1,0:T(8,128)(2,1)}, u32[]{:S(2)}) copy-start(bf16[64,32,256]{2,1,0:T(8,128)(2,1)} %param.16) | copy-start | bytes 3145732
  7.2 12.6 %copy-start.46 = (bf16[8,32,4]{1,2,0:T(4,128)(2,1)S(1)}, bf16[8,32,4]{1,2,0:T(4,128)(2,1)}, u32[]{:S(2)}) copy-start(bf16[8,32,4]{1,2,0:T(4,128)(2,1)} %param.17) | copy-start | bytes 6148
  7.2 12.6 %copy-start.47 = (s32[1,4]{1,0:T(1,128)S(1)}, s32[1,4]{1,0:T(1,128)}, u32[]{:S(2)}) copy-start(s32[1,4]{1,0:T(1,128)} %param.22) | copy-start | bytes 52
  7.2 12.8 %copy-start.48 = (s32[1,4]{1,0:T(1,128)S(1)}, s32[1,4]{1,0:T(1,128)}, u32[]{:S(2)}) copy-start(s32[1,4]{1,0:T(1,128)} %param.21) | copy-start | bytes 52
  7.2 101.8 %all-gather.2.cloned.1.call-start = ((), (), s32[]{:S(2)}) async-start(), calls=%async_computation.1 | async-start | bytes 2228224 | tf_op jit(solution)/shard_map/all_gather | solution.py:109
  12.9 17.6 %collective-permute-start.11 = (bf16[64,1,256]{0,1,2:T(2,128)(2,1)}, bf16[64,1,256]{0,1,2:T(2,128)(2,1)S(1)}, u32[]{:S(2)}, u32[]{:S(2)}) collective-permute-start(bf16[64,1,256]{0,1,2:T(2,128)(2,1)} %get-tuple-element.73), channel_id=1, source_target_pairs={{16,0},{32,16},{48,32},{64,48},{80,64},{96,80},{112,96},{17,1},{33... | collective-permute-start | bytes 98312 | tf_op jit(solution)/shard_map/ppermute | solution.py:20
  16.2 14.3 %collective-permute-start.10 = (bf16[64,1,256]{0,1,2:T(2,128)(2,1)}, bf16[64,1,256]{0,1,2:T(2,128)(2,1)S(1)}, u32[]{:S(2)}, u32[]{:S(2)}) collective-permute-start(bf16[64,1,256]{0,1,2:T(2,128)(2,1)} %get-tuple-element.72), channel_id=1, source_target_pairs={{0,16},{16,32},{32,48},{48,64},{64,80},{80,96},{96,112},{1,17},{17... | collective-permute-start | bytes 98312 | tf_op jit(solution)/shard_map/ppermute | solution.py:18
  19.8 413.5 %all-reduce.3.cloned.1.call-start = ((), (), s32[]{:S(2)}) async-start(), calls=%async_computation.3 | async-start | bytes 1179648 | tf_op jit(solution)/shard_map/psum | solution.py:141
  20.0 101.0 %copy-start.44 = (bf16[4,32,4,1]{1,0,2,3:T(4,128)(2,1)}, bf16[4,32,4,1]{1,0,2,3:T(4,128)(2,1)S(1)}, u32[]{:S(2)}) copy-start(bf16[4,32,4,1]{1,0,2,3:T(4,128)(2,1)S(1)} %fusion.70) | copy-start | bytes 3076
  31.2 13.6 %collective-permute-start.12 = (bf16[64,34,1]{0,1,2:T(8,128)(2,1)}, bf16[64,34,1]{0,1,2:T(8,128)(2,1)S(1)}, u32[]{:S(2)}, u32[]{:S(2)}) collective-permute-start(bf16[64,34,1]{0,1,2:T(8,128)(2,1)} %get-tuple-element.68), channel_id=1, source_target_pairs={{1,0},{2,1},{3,2},{4,3},{5,4},{6,5},{7,6},{8,7},{9,8},{10,9},{11,1... | collective-permute-start | bytes 13064 | tf_op jit(solution)/shard_map/ppermute | solution.py:20
  32.4 12.3 %collective-permute-start.13 = (bf16[64,34,1]{0,1,2:T(8,128)(2,1)}, bf16[64,34,1]{0,1,2:T(8,128)(2,1)}, u32[]{:S(2)}, u32[]{:S(2)}) collective-permute-start(bf16[64,34,1]{0,1,2:T(8,128)(2,1)} %get-tuple-element.69), channel_id=1, source_target_pairs={{0,1},{1,2},{2,3},{3,4},{4,5},{5,6},{6,7},{7,8},{8,9},{9,10},{10,1... | collective-permute-start | bytes 13064 | tf_op jit(solution)/shard_map/ppermute | solution.py:18
  110.2 7.6 %collective-permute-start.1 = (bf16[8,64,128]{2,1,0:T(8,128)(2,1)S(1)}, bf16[8,64,128]{2,1,0:T(8,128)(2,1)S(1)}, u32[]{:S(2)}, u32[]{:S(2)}) collective-permute-start(bf16[8,64,128]{2,1,0:T(8,128)(2,1)S(1)} %get-tuple-element.75), channel_id=1, source_target_pairs={{16,0},{32,16},{48,32},{64,48},{80,64},{96,80},{112,96},{17,1},{33... | collective-permute-start | bytes 393224 | tf_op jit(solution)/shard_map/ppermute | solution.py:20
  112.1 5.7 %collective-permute-start = (bf16[8,64,128]{2,1,0:T(8,128)(2,1)S(1)}, bf16[8,64,128]{2,1,0:T(8,128)(2,1)S(1)}, u32[]{:S(2)}, u32[]{:S(2)}) collective-permute-start(bf16[8,64,128]{2,1,0:T(8,128)(2,1)S(1)} %get-tuple-element.74), channel_id=1, source_target_pairs={{0,16},{16,32},{32,48},{48,64},{64,80},{80,96},{96,112},{1,17},{17... | collective-permute-start | bytes 393224 | tf_op jit(solution)/shard_map/ppermute | solution.py:18
  118.8 11.2 %copy-start.30 = (bf16[8,8,32,256]{3,1,2,0:T(8,128)(2,1)S(1)}, bf16[8,8,32,256]{3,1,2,0:T(8,128)(2,1)}, u32[]{:S(2)}) copy-start(bf16[8,8,32,256]{3,1,2,0:T(8,128)(2,1)} %copy.392) | copy-start | bytes 3145732
  123.6 12.7 %collective-permute-start.3 = (bf16[80,1,256]{2,1,0:T(2,128)(2,1)S(1)}, bf16[80,1,256]{2,1,0:T(2,128)(2,1)S(1)}, u32[]{:S(2)}, u32[]{:S(2)}) collective-permute-start(bf16[80,1,256]{2,1,0:T(2,128)(2,1)S(1)} %get-tuple-element.98), channel_id=1, source_target_pairs={{16,0},{32,16},{48,32},{64,48},{80,64},{96,80},{112,96},{17,1},{33... | collective-permute-start | bytes 122888 | tf_op jit(solution)/shard_map/ppermute | solution.py:20
  125.5 10.7 %collective-permute-start.2 = (bf16[80,1,256]{2,1,0:T(2,128)(2,1)S(1)}, bf16[80,1,256]{2,1,0:T(2,128)(2,1)S(1)}, u32[]{:S(2)}, u32[]{:S(2)}) collective-permute-start(bf16[80,1,256]{2,1,0:T(2,128)(2,1)S(1)} %get-tuple-element.97), channel_id=1, source_target_pairs={{0,16},{16,32},{32,48},{48,64},{64,80},{80,96},{96,112},{1,17},{17... | collective-permute-start | bytes 122888 | tf_op jit(solution)/shard_map/ppermute | solution.py:18
  140.3 14.4 %collective-permute-start.5 = (bf16[80,34,1]{0,1,2:T(8,128)(2,1)S(1)}, bf16[80,34,1]{0,1,2:T(8,128)(2,1)S(1)}, u32[]{:S(2)}, u32[]{:S(2)}) collective-permute-start(bf16[80,34,1]{0,1,2:T(8,128)(2,1)S(1)} %copy.294), channel_id=1, source_target_pairs={{1,0},{2,1},{3,2},{4,3},{5,4},{6,5},{7,6},{8,7},{9,8},{10,9},{11,1... | collective-permute-start | bytes 16328 | tf_op jit(solution)/shard_map/ppermute | solution.py:20
  142.1 13.1 %collective-permute-start.4 = (bf16[80,34,1]{0,1,2:T(8,128)(2,1)S(1)}, bf16[80,34,1]{0,1,2:T(8,128)(2,1)S(1)}, u32[]{:S(2)}, u32[]{:S(2)}) collective-permute-start(bf16[80,34,1]{0,1,2:T(8,128)(2,1)S(1)} %copy.292), channel_id=1, source_target_pairs={{0,1},{1,2},{2,3},{3,4},{4,5},{5,6},{6,7},{7,8},{8,9},{9,10},{10,1... | collective-permute-start | bytes 16328 | tf_op jit(solution)/shard_map/ppermute | solution.py:18
  181.0 60.0 %copy-start.1 = (bf16[64,32,256]{2,0,1:T(8,128)(2,1)}, bf16[64,32,256]{2,0,1:T(8,128)(2,1)S(1)}, u32[]{:S(2)}) copy-start(bf16[64,32,256]{2,0,1:T(8,128)(2,1)S(1)} %get-tuple-element.71) | copy-start | bytes 3145732
  197.9 11.9 %collective-permute-start.7 = (bf16[64,1,256]{2,0,1:T(8,128)(2,1)S(1)}, bf16[64,1,256]{2,0,1:T(8,128)(2,1)S(1)}, u32[]{:S(2)}, u32[]{:S(2)}) collective-permute-start(bf16[64,1,256]{2,0,1:T(8,128)(2,1)S(1)} %get-tuple-element.120), channel_id=1, source_target_pairs={{16,0},{32,16},{48,32},{64,48},{80,64},{96,80},{112,96},{17,1},{33... | collective-permute-start | bytes 98312 | tf_op jit(solution)/shard_map/ppermute | solution.py:20
  199.8 10.0 %collective-permute-start.6 = (bf16[64,1,256]{2,0,1:T(8,128)(2,1)S(1)}, bf16[64,1,256]{2,0,1:T(8,128)(2,1)S(1)}, u32[]{:S(2)}, u32[]{:S(2)}) collective-permute-start(bf16[64,1,256]{2,0,1:T(8,128)(2,1)S(1)} %get-tuple-element.119), channel_id=1, source_target_pairs={{0,16},{16,32},{32,48},{48,64},{64,80},{80,96},{96,112},{1,17},{17... | collective-permute-start | bytes 98312 | tf_op jit(solution)/shard_map/ppermute | solution.py:18
  203.5 17.6 %collective-permute-start.15 = (bf16[64,1,256]{2,0,1:T(8,128)(2,1)}, bf16[64,1,256]{2,0,1:T(8,128)(2,1)S(1)}, u32[]{:S(2)}, u32[]{:S(2)}) collective-permute-start(bf16[64,1,256]{2,0,1:T(8,128)(2,1)} %get-tuple-element.114), channel_id=1, source_target_pairs={{16,0},{32,16},{48,32},{64,48},{80,64},{96,80},{112,96},{17,1},{33... | collective-permute-start | bytes 98312 | tf_op jit(solution)/shard_map/ppermute | solution.py:20
  205.4 15.7 %collective-permute-start.14 = (bf16[64,1,256]{2,0,1:T(8,128)(2,1)S(1)}, bf16[64,1,256]{2,0,1:T(8,128)(2,1)S(1)}, u32[]{:S(2)}, u32[]{:S(2)}) collective-permute-start(bf16[64,1,256]{2,0,1:T(8,128)(2,1)S(1)} %get-tuple-element.113), channel_id=1, source_target_pairs={{0,16},{16,32},{32,48},{48,64},{64,80},{80,96},{96,112},{1,17},{17... | collective-permute-start | bytes 98312 | tf_op jit(solution)/shard_map/ppermute | solution.py:18
  213.2 24.1 %collective-permute-start.9 = (bf16[64,34,1]{0,1,2:T(8,128)(2,1)}, bf16[64,34,1]{0,1,2:T(8,128)(2,1)}, u32[]{:S(2)}, u32[]{:S(2)}) collective-permute-start(bf16[64,34,1]{0,1,2:T(8,128)(2,1)} %copy.302), channel_id=1, source_target_pairs={{1,0},{2,1},{3,2},{4,3},{5,4},{6,5},{7,6},{8,7},{9,8},{10,9},{11,1... | collective-permute-start | bytes 13064 | tf_op jit(solution)/shard_map/ppermute | solution.py:20
  216.5 22.7 %collective-permute-start.8 = (bf16[64,34,1]{0,1,2:T(8,128)(2,1)}, bf16[64,34,1]{0,1,2:T(8,128)(2,1)}, u32[]{:S(2)}, u32[]{:S(2)}) collective-permute-start(bf16[64,34,1]{0,1,2:T(8,128)(2,1)} %copy.298), channel_id=1, source_target_pairs={{0,1},{1,2},{2,3},{3,4},{4,5},{5,6},{6,7},{7,8},{8,9},{9,10},{10,1... | collective-permute-start | bytes 13064 | tf_op jit(solution)/shard_map/ppermute | solution.py:18
  224.4 30.5 %collective-permute-start.17 = (bf16[64,34,1]{0,1,2:T(8,128)(2,1)}, bf16[64,34,1]{0,1,2:T(8,128)(2,1)}, u32[]{:S(2)}, u32[]{:S(2)}) collective-permute-start(bf16[64,34,1]{0,1,2:T(8,128)(2,1)} %copy.345), channel_id=1, source_target_pairs={{0,1},{1,2},{2,3},{3,4},{4,5},{5,6},{6,7},{7,8},{8,9},{9,10},{10,1... | collective-permute-start | bytes 13064 | tf_op jit(solution)/shard_map/ppermute | solution.py:18
  230.5 25.5 %collective-permute-start.16 = (bf16[64,34,1]{0,1,2:T(8,128)(2,1)}, bf16[64,34,1]{0,1,2:T(8,128)(2,1)}, u32[]{:S(2)}, u32[]{:S(2)}) collective-permute-start(bf16[64,34,1]{0,1,2:T(8,128)(2,1)} %copy.341), channel_id=1, source_target_pairs={{1,0},{2,1},{3,2},{4,3},{5,4},{6,5},{7,6},{8,7},{9,8},{10,9},{11,1... | collective-permute-start | bytes 13064 | tf_op jit(solution)/shard_map/ppermute | solution.py:20
  243.4 9.6 %copy-start.5 = (bf16[64,34,257]{2,0,1:T(8,128)(2,1)}, bf16[64,34,257]{2,0,1:T(8,128)(2,1)S(1)}, u32[]{:S(2)}) copy-start(bf16[64,34,257]{2,0,1:T(8,128)(2,1)S(1)} %get-tuple-element.108) | copy-start | bytes 3355396
  274.6 5.6 %collective-permute-start.18 = (bf16[8,64,128]{2,0,1:T(8,128)(2,1)S(1)}, bf16[8,64,128]{2,0,1:T(8,128)(2,1)S(1)}, u32[]{:S(2)}, u32[]{:S(2)}) collective-permute-start(bf16[8,64,128]{2,0,1:T(8,128)(2,1)S(1)} %get-tuple-element.93), channel_id=1, source_target_pairs={{0,16},{16,32},{32,48},{48,64},{64,80},{80,96},{96,112},{1,17},{17... | collective-permute-start | bytes 393224 | tf_op jit(solution)/shard_map/ppermute | solution.py:30
  277.4 6.3 %collective-permute-start.19 = (bf16[8,64,128]{2,0,1:T(8,128)(2,1)S(1)}, bf16[8,64,128]{2,0,1:T(8,128)(2,1)S(1)}, u32[]{:S(2)}, u32[]{:S(2)}) collective-permute-start(bf16[8,64,128]{2,0,1:T(8,128)(2,1)S(1)} %get-tuple-element.92), channel_id=1, source_target_pairs={{16,0},{32,16},{48,32},{64,48},{80,64},{96,80},{112,96},{17,1},{33... | collective-permute-start | bytes 393224 | tf_op jit(solution)/shard_map/ppermute | solution.py:30
  280.2 231.6 %reduce-scatter.2.cloned.1.call-start = ((), (), s32[]{:S(2)}) async-start(), calls=%async_computation.2 | async-start | bytes 4456448 | tf_op jit(solution)/shard_map/reduce_scatter | solution.py:169
  (40 other events, 113.7 us)
Sparse Core Ops, SparseCore 0:
  19.9 45.3 all-gather.1
  280.3 152.9 all-reduce.2
  437.5 74.2 reduce-scatter.1
where the time goes:
time: 529 us; the launch traced here: 520 us
  waiting for transfers between devices  192 us (36%)
  local copies, waits for them, and re-layouts  155 us (29%)
  matrix products  65.3 us (12%)
  starting transfers between devices  57 us (11%)
  other arithmetic  27.5 us (5%)
  between operations  23.8 us (4%)
    psum x1, waiting for transfers between devices, local(): lax.psum((first_local, second_local), ('row', 'col'))  113 us
    reduce_scatter x1, waiting for transfers between devices, local(): lax.psum_scatter(spread, 'col', scatter_dimension=0, tiled=True)  76.7 us
    unnamed x125, local copies, waits for them, and re-layouts  58.8 us
    slice x8, local copies, waits for them, and re-layouts, shifted(): padded[:, row_off:row_off + tile_rows, col_off:col_off + tile_cols]  37.1 us
    ppermute x9, starting transfers between devices, with_halo(): lax.ppermute(tail, axis, [(i, (i + 1) % count) for i in range(ends)])  36.1 us
    dot_general x18, matrix products, weight_grad(): lax.dot_general(flat, shifted(padded, row_off, col_off, tile_rows, tile_c...  30.9 us
    dot_general x18, matrix products, conv_adjoint(): lax.dot_general(weights[row_off, col_off], shifted(padded, 2 - row_off, 2...  23.2 us
    concatenate x10, other arithmetic, with_halo(): jnp.concatenate([lax.ppermute(tail, axis, [(i, (i + 1) % count) for i in...  21 us
  transfers between devices with their start and end apart: 23, of which 3 were waited for; matrix products, arithmetic and copies ran while one was open for 31% of the time, Pallas kernels for 0%

commit v1 on v0

v1 whole, which is shorter than its diff:
```python
import jax
import jax.numpy as jnp
from jax import lax
from jax.experimental import pallas as pl
from jax.experimental.pallas import tpu as pltpu
from jax.sharding import PartitionSpec as P

F32 = jnp.float32
BF16 = jnp.bfloat16
MESH = pl.DeviceIdType.MESH

NR = 8
NC = 16
HB = 2
K = 4
FR = 32
CH = 64
FS = 16
CIN = 80
CW = 128
NB = NC + 2 * HB

DIRS = ((0, 1), (0, -1), (1, 1), (1, -1), (-1, 1), (-1, -1))
COT, INP, HID, ACT = range(4)


def iota(shape, dim):
    return lax.broadcasted_iota(jnp.int32, shape, dim)


def dot(a, b):
    return jnp.dot(a, b, preferred_element_type=F32)


def dot_nt(a, b):
    return lax.dot_general(a, b, (((1,), (1,)), ((), ())), preferred_element_type=F32)


def kernel(
    block_ids,
    weight_ids,
    col_start,
    coarse,
    noisy,
    cot,
    rowsx,
    cols,
    wf1,
    wf2,
    wb1,
    wb2,
    fine_out,
    first_out,
    second_out,
    coarse_out,
    v_cot,
    v_in,
    v_hid,
    v_act,
    hgrad,
    edge,
    edge_in,
    edge_got,
    edge_got_in,
    halo,
    cs,
    slab,
    gath,
    pieces,
    lmat,
    sec,
    pgrad,
    sbuf,
    rbuf,
    acc1,
    acc2,
    gbuf,
    gpart,
    grow,
    gall,
    x_send,
    x_recv,
    cs_send,
    cs_recv,
    ag_send,
    ag_recv,
    hb_send,
    rs_send,
    rs_recv,
    w1_send,
    w1_recv,
    w2_send,
    w2_recv,
    w3_send,
    w3_recv,
):
    r = lax.axis_index("row")
    c = lax.axis_index("col")

    def row_at(d):
        return lax.rem(r + (d + NR), NR)

    def col_at(d):
        return lax.rem(c + (d + NC), NC)

    def remote(src, dst, send, recv, device):
        return pltpu.make_async_remote_copy(
            src_ref=src, dst_ref=dst, send_sem=send, recv_sem=recv, device_id=device, device_id_type=MESH
        )

    barrier = pltpu.get_barrier_semaphore()

    def greet_cols(d, _):
        for dr in (-1, 0, 1):
            if dr == 0:
                @pl.when(d > 0)
                def _():
                    pl.semaphore_signal(barrier, inc=1, device_id=(r, col_at(d)), device_id_type=MESH)
            else:
                pl.semaphore_signal(barrier, inc=1, device_id=(row_at(dr), col_at(d)), device_id_type=MESH)
        return 0

    lax.fori_loop(0, NC, greet_cols, 0)
    for dr in range(2, NR - 1):
        pl.semaphore_signal(barrier, inc=1, device_id=(row_at(dr), c), device_id_type=MESH)
    pl.semaphore_wait(barrier, 3 * NC - 1 + NR - 3)

    cs[c] = jnp.full((8, 128), col_start[0], jnp.int32)

    def cs_copy(d):
        return remote(cs.at[c], cs.at[c], cs_send.at[d], cs_recv.at[c], (r, col_at(d)))

    def cs_arrival(d):
        other = col_at(d)
        return remote(cs.at[other], cs.at[other], cs_send.at[d], cs_recv.at[other], (r, other))

    def start_cs(d, _):
        cs_copy(d).start()
        return 0

    lax.fori_loop(1, NC, start_cs, 0)

    i0, i1 = iota((256, 256), 0), iota((256, 256), 1)
    perm = jnp.where(
        (lax.rem(i0, 16) == lax.div(i1, 16)) & (lax.div(i0, 16) == lax.rem(i1, 16)), 1.0, 0.0
    ).astype(BF16)

    def flip_in(src, dst, c0, h0):
        block = src[c0 : c0 + 16, h0 : h0 + 16, :].reshape(256, 256)
        moved = dot(perm, block).astype(BF16).reshape(16, 16, 256)
        dst[1 + h0 : 17 + h0, 1, c0 : c0 + 16, :] = moved

    for c0 in range(0, CH, 16):
        for h0 in range(0, FR, 16):
            flip_in(cot, v_cot, c0, h0)

    bufs = {
        COT: (v_cot, edge.at[0], edge_got.at[0], CH),
        INP: (v_in, edge_in, edge_got_in, CIN),
        HID: (v_hid, edge.at[1], edge_got.at[1], CH),
        ACT: (v_act, edge.at[2], edge_got.at[2], CH),
    }

    def halo_copies(x):
        v, e, got, _ = bufs[x]
        copies = [
            remote(e, got.at[i], x_send.at[x, i], x_recv.at[x, i], (row_at(dr), col_at(dc)))
            for i, (dr, dc) in enumerate(DIRS)
        ]
        copies.append(remote(v.at[FR, 1], v.at[0, 1], x_send.at[x, 6], x_recv.at[x, 6], (row_at(1), c)))
        copies.append(remote(v.at[1, 1], v.at[FR + 1, 1], x_send.at[x, 7], x_recv.at[x, 7], (row_at(-1), c)))
        return copies

    def halo_start(x):
        v, e, _, chans = bufs[x]
        lane = iota((chans, 128), 1)

        def pack(h, held):
            left = v[h + 1, 1, :, 0:128].astype(F32)[:, 0:1]
            right = v[h + 1, 1, :, 128:256].astype(F32)[:, 127:128]
            held = jnp.where(lane == h, left, held)
            return jnp.where(lane == h + 64, right, held)

        e[...] = lax.fori_loop(0, FR, pack, jnp.zeros((chans, 128), F32)).astype(BF16)
        for copy in halo_copies(x):
            copy.start()

    def halo_finish(x):
        v, _, got, chans = bufs[x]
        for copy in halo_copies(x):
            copy.wait()
        lane = iota((chans, 128), 1)

        @pl.when(r == 0)
        def _():
            v[0, 1] = jnp.zeros((chans, 256), BF16)

        @pl.when(r == NR - 1)
        def _():
            v[FR + 1, 1] = jnp.zeros((chans, 256), BF16)

        top = (r > 0).astype(F32)
        bottom = (r < NR - 1).astype(F32)
        west = (c > 0).astype(F32)
        east = (c < NC - 1).astype(F32)

        def side(mid, up, down, s_mid, s_up, s_down, there):
            a = pltpu.roll(got[mid].astype(F32), s_mid, 1)
            b = pltpu.roll(got[up].astype(F32), s_up, 1) * top
            d = pltpu.roll(got[down].astype(F32), s_down, 1) * bottom
            return jnp.where(lane == 0, b, jnp.where(lane == FR + 1, d, a)) * there

        halo[0, 0:chans] = side(0, 2, 4, 65, 33, 97, west)
        halo[1, 0:chans] = side(1, 3, 5, 1, 97, 33, east)

        def shift(j, _):
            t0 = v[j, 1, :, 0:128].astype(F32)
            t1 = v[j, 1, :, 128:256].astype(F32)
            w = pltpu.roll(halo[0, 0:chans], lax.rem(128 - j, 128), 1)
            e = pltpu.roll(halo[1, 0:chans], 127 - j, 1)
            r0, r1 = pltpu.roll(t0, 1, 1), pltpu.roll(t1, 1, 1)
            s0, s1 = pltpu.roll(t0, 127, 1), pltpu.roll(t1, 127, 1)
            v[j, 0, :, 0:128] = jnp.where(lane == 0, w, r0).astype(BF16)
            v[j, 0, :, 128:256] = jnp.where(lane == 0, r0, r1).astype(BF16)
            v[j, 2, :, 0:128] = jnp.where(lane == 127, s1, s0).astype(BF16)
            v[j, 2, :, 128:256] = jnp.where(lane == 127, e, s1).astype(BF16)
            return 0

        lax.fori_loop(0, FR + 2, shift, 0)

    def conv_pair(weights, v, p, chans):
        return dot(weights[...], v[pl.ds(2 * p, 4)].reshape(12 * chans, 256))

    halo_start(COT)

    for h0 in range(0, FR, 16):
        flip_in(noisy, v_in, 0, h0)

    def wait_cs(d, _):
        cs_copy(d).wait_send()
        cs_arrival(d).wait_recv()
        return 0

    lax.fori_loop(1, NC, wait_cs, 0)

    def ag_copy(d):
        to = col_at(d)
        return remote(slab.at[to], gath.at[HB + c], ag_send.at[d], ag_recv.at[HB + c], (r, to))

    def hb_copy(n, down):
        if down:
            return remote(slab.at[n], gath.at[c - (NC - HB)], hb_send.at[n], ag_recv.at[c - (NC - HB)], (row_at(1), n))
        return remote(slab.at[n], gath.at[NC + HB + c], hb_send.at[n], ag_recv.at[NC + HB + c], (row_at(-1), n))

    whole = coarse[...].reshape(256, 256)

    def cut(d, _):
        to = col_at(d)
        start = cs[to][0:1, :]
        pick = jnp.where(iota((256, 128), 0) == iota((256, 128), 1) + start, 1.0, 0.0).astype(BF16)
        slab[to] = dot(whole, pick).astype(BF16).reshape(4, CH, CW)

        @pl.when(d > 0)
        def _():
            ag_copy(d).start()

        @pl.when(d == 0)
        def _():
            gath[HB + c] = slab[c]

        @pl.when(c >= NC - HB)
        def _():
            hb_copy(to, True).start()

        @pl.when(c < HB)
        def _():
            hb_copy(to, False).start()

        return 0

    lax.fori_loop(0, NC, cut, 0)

    halo_finish(COT)

    def hidden_grad(p, _):
        hgrad[pl.ds(2 * p, 2)] = conv_pair(wb2, v_cot, p, CH).reshape(2, CH, 256)
        return 0

    lax.fori_loop(0, FR // 2, hidden_grad, 0)

    lane256 = iota((FR, 256), 1)
    table = jnp.zeros((FR, 256), BF16)
    for k in range(K):
        table = jnp.where(lax.div(lane256, 64) == k, rowsx[weight_ids[0, k]], table)
    spread = jnp.where(lax.div(iota((512, FR), 0), 16) == iota((512, FR), 1), 1.0, 0.0).astype(BF16)
    same = lax.rem(iota((512, 256), 0), 16) == lax.rem(iota((512, 256), 1), 16)
    lmat[...] = jnp.where(same, dot(spread, table), 0.0).astype(BF16)

    def wait_ag(d, _):
        ag_copy(d).wait_send()
        remote(slab.at[0], gath.at[HB + col_at(d)], ag_send.at[d], ag_recv.at[HB + col_at(d)], (r, col_at(d))).wait_recv()
        return 0

    lax.fori_loop(1, NC, wait_ag, 0)
    for b in (0, 1, NB - 2, NB - 1):
        remote(slab.at[0], gath.at[b], hb_send.at[0], ag_recv.at[b], (row_at(1), c)).wait_recv()

    def wait_hb(n, _):
        @pl.when((c >= NC - HB) | (c < HB))
        def _():
            remote(slab.at[n], gath.at[0], hb_send.at[n], ag_recv.at[0], (row_at(1), n)).wait_send()

        return 0

    lax.fori_loop(0, NC, wait_hb, 0)

    first_block = r * NC - HB
    for k in range(K):
        piece = gath[jnp.clip(block_ids[0, k] - first_block, 0, NB - 1)]
        for g in range(4):
            pieces[g, 64 * k : 64 * k + 64, :] = piece[:, 16 * g : 16 * g + 16, :].reshape(64, CW)
    for g in range(4):
        sec[:, 16 * g : 16 * g + 16, :] = dot(lmat[...], pieces[g]).astype(BF16).reshape(FR, 16, CW)

    def regrid(q, _):
        rows = sec[pl.ds(4 * q, 4)].reshape(256, CW)
        v_in[pl.ds(1 + 4 * q, 4), 1, FS:CIN, :] = dot(rows, cols[...]).astype(BF16).reshape(4, CH, 256)
        return 0

    lax.fori_loop(0, FR // 4, regrid, 0)

    halo_start(INP)
    halo_finish(INP)

    def first_level(p, _):
        pre = conv_pair(wf1, v_in, p, CIN).reshape(2, CH, 256)
        s = 1.0 / (1.0 + jnp.exp(-pre))
        v_hid[pl.ds(1 + 2 * p, 2), 1] = (pre * s).astype(BF16)
        slope = s * (1.0 + pre * (1.0 - s))
        v_act[pl.ds(1 + 2 * p, 2), 1] = (hgrad[pl.ds(2 * p, 2)] * slope).astype(BF16)
        return 0

    lax.fori_loop(0, FR // 2, first_level, 0)
    halo_start(HID)
    halo_start(ACT)

    def weight_grad(acc, left, v, chans):
        acc[...] = jnp.zeros(acc.shape, F32)

        def step(p, _):
            rows = left[pl.ds(1 + 2 * p, 2), 1].reshape(128, 256)
            for j in range(4):
                acc[j, :, 0 : 3 * chans] += dot_nt(rows, v[2 * p + j].reshape(3 * chans, 256))
            return 0

        lax.fori_loop(0, FR // 2, step, 0)

    weight_grad(acc1, v_act, v_in, CIN)
    halo_finish(HID)
    weight_grad(acc2, v_cot, v_hid, CH)
    for which, acc in ((0, acc1), (1, acc2)):
        for a in range(3):
            total = acc[a, 0:64, :] + acc[a + 1, 64:128, :]
            gbuf[8 * which : 8 * which + 8, a] = total.reshape(8, 8, 256)

    def w1_copy(d):
        to = col_at(d)
        return remote(gbuf.at[to], gpart.at[c], w1_send.at[d], w1_recv.at[c], (r, to))

    def start_w1(d, _):
        w1_copy(d).start()
        return 0

    lax.fori_loop(1, NC, start_w1, 0)
    gpart[c] = gbuf[c]

    halo_finish(ACT)

    def cond_grad(p, _):
        grad = conv_pair(wb1, v_act, p, CH).astype(BF16)
        sec[pl.ds(2 * p, 2)] = dot_nt(grad, cols[...]).astype(BF16).reshape(2, CH, CW)
        return 0

    lax.fori_loop(0, FR // 2, cond_grad, 0)
    eye = jnp.where(i0 == i1, 1.0, 0.0).astype(BF16)
    lmat_t = dot_nt(eye, lmat[...]).astype(BF16)
    for g in range(4):
        part = dot(lmat_t, sec[:, 16 * g : 16 * g + 16, :].reshape(512, CW))
        pgrad[:, :, 16 * g : 16 * g + 16, :] = part.reshape(K, 4, 16, CW)

    def contribution(b):
        total = None
        for k in range(K):
            hit = (block_ids[0, k] - first_block == b).astype(F32)
            term = pgrad[k] * hit
            total = term if total is None else total + term
        return total.astype(BF16)

    def rs_copy(d):
        to = col_at(d)
        return remote(sbuf.at[HB + to], rbuf.at[c], rs_send.at[d], rs_recv.at[c], (r, to))

    def rs_halo(n):
        b, dr, to = ((0, -1, NC - 2), (1, -1, NC - 1), (NB - 2, 1, 0), (NB - 1, 1, 1))[n]
        return remote(sbuf.at[b], rbuf.at[NC + c], rs_send.at[NC + n], rs_recv.at[NC + c], (row_at(dr), to))

    for n, b in enumerate((0, 1, NB - 2, NB - 1)):
        sbuf[b] = contribution(b)
        rs_halo(n).start()

    def send_grad(d, _):
        to = col_at(d)
        sbuf[HB + to] = contribution(HB + to)

        @pl.when(d > 0)
        def _():
            rs_copy(d).start()

        @pl.when(d == 0)
        def _():
            rbuf[c] = sbuf[HB + c]

        return 0

    lax.fori_loop(0, NC, send_grad, 0)

    def wait_w1(d, _):
        w1_copy(d).wait_send()
        other = col_at(d)
        remote(gbuf.at[other], gpart.at[other], w1_send.at[d], w1_recv.at[other], (r, other)).wait_recv()
        return 0

    lax.fori_loop(1, NC, wait_w1, 0)
    total = gpart[0]
    for n in range(1, NC):
        total = total + gpart[n]
    grow[r] = total

    def w2_copy(d):
        return remote(grow.at[r], grow.at[r], w2_send.at[d], w2_recv.at[r], (row_at(d), c))

    for d in range(1, NR):
        w2_copy(d).start()

    def second_level(p, _):
        hgrad[pl.ds(2 * p, 2)] = conv_pair(wf2, v_hid, p, CH).reshape(2, CH, 256)
        return 0

    lax.fori_loop(0, FR // 2, second_level, 0)

    for d in range(1, NR):
        w2_copy(d).wait_send()
        other = row_at(d)
        remote(grow.at[other], grow.at[other], w2_send.at[d], w2_recv.at[other], (other, c)).wait_recv()
    total = grow[0]
    for n in range(1, NR):
        total = total + grow[n]
    gall[c] = total

    def w3_copy(d):
        return remote(gall.at[c], gall.at[c], w3_send.at[d], w3_recv.at[c], (r, col_at(d)))

    def start_w3(d, _):
        w3_copy(d).start()
        return 0

    lax.fori_loop(1, NC, start_w3, 0)

    for c0 in range(0, CH, 16):
        for h0 in range(0, FR, 16):
            block = hgrad[h0 : h0 + 16, c0 : c0 + 16, :].astype(BF16).reshape(256, 256)
            fine_out[c0 : c0 + 16, h0 : h0 + 16, :] = dot(perm, block).astype(BF16).reshape(16, 16, 256)

    def place(n, _):
        other = col_at(n)

        @pl.when(n > 0)
        def _():
            rs_copy(n).wait_send()
            remote(sbuf.at[0], rbuf.at[other], rs_send.at[n], rs_recv.at[other], (r, other)).wait_recv()

        return 0

    lax.fori_loop(0, NC, place, 0)
    for n in range(4):
        rs_halo(n).wait_send()
    outer = (c < HB) | (c >= NC - HB)

    def add_from(base):
        def add(n, held):
            start = cs[n][0:1, :]
            start = jnp.concatenate([start, start], axis=1)
            spot = jnp.where(iota((CW, 256), 1) == iota((CW, 256), 0) + start, 1.0, 0.0).astype(BF16)
            coarse_out[...] += dot(rbuf[base + n].reshape(256, CW), spot).reshape(4, CH, 256)
            return 0

        lax.fori_loop(0, NC, add, 0)

    coarse_out[...] = jnp.zeros((4, CH, 256), F32)
    add_from(0)

    @pl.when(outer)
    def _():
        def wait(n, _):
            remote(sbuf.at[0], rbuf.at[NC + n], rs_send.at[0], rs_recv.at[NC + n], (row_at(1), n)).wait_recv()
            return 0

        lax.fori_loop(0, NC, wait, 0)
        add_from(NC)

    def wait_w3(d, _):
        w3_copy(d).wait_send()
        other = col_at(d)
        remote(gall.at[other], gall.at[other], w3_send.at[d], w3_recv.at[other], (r, other)).wait_recv()
        return 0

    lax.fori_loop(1, NC, wait_w3, 0)
    for a in range(3):
        for e in range(3):
            for og in range(8):
                first_out[a, e, 8 * og : 8 * og + 8, :] = gall[og, a, :, e * CIN : (e + 1) * CIN]
                second_out[a, e, 8 * og : 8 * og + 8, :] = gall[8 + og, a, :, e * CH : (e + 1) * CH]


def pair_matrix(w):
    outs, ins = w.shape[2], w.shape[3]
    flat = w.transpose(2, 0, 1, 3).reshape(outs, 9 * ins)
    none = jnp.zeros((outs, 3 * ins), w.dtype)
    return jnp.concatenate(
        [jnp.concatenate([flat, none], axis=1), jnp.concatenate([none, flat], axis=1)], axis=0
    )


def adjoint(w):
    return w[::-1, ::-1].transpose(0, 1, 3, 2)


def local(
    coarse,
    noisy,
    cotangent,
    interp_rows,
    interp_cols,
    first_weight,
    second_weight,
    block_ids,
    weight_ids,
    col_start,
):
    rowsx = jnp.tile(jnp.repeat(interp_rows, 16, axis=2), (1, 1, K))
    smem = pl.BlockSpec(memory_space=pltpu.SMEM)
    vmem = pl.BlockSpec(memory_space=pltpu.VMEM)
    dma = pltpu.SemaphoreType.DMA
    return pl.pallas_call(
        kernel,
        out_shape=(
            jax.ShapeDtypeStruct((CH, FR, 256), BF16),
            jax.ShapeDtypeStruct((3, 3, CH, CIN), F32),
            jax.ShapeDtypeStruct((3, 3, CH, CH), F32),
            jax.ShapeDtypeStruct((4, CH, 256), F32),
        ),
        in_specs=[smem] * 3 + [vmem] * 9,
        out_specs=(vmem,) * 4,
        scratch_shapes=[
            pltpu.VMEM((FR + 2, 3, CH, 256), BF16),
            pltpu.VMEM((FR + 2, 3, CIN, 256), BF16),
            pltpu.VMEM((FR + 2, 3, CH, 256), BF16),
            pltpu.VMEM((FR + 2, 3, CH, 256), BF16),
            pltpu.VMEM((FR, CH, 256), F32),
            pltpu.VMEM((3, CH, 128), BF16),
            pltpu.VMEM((CIN, 128), BF16),
            pltpu.VMEM((3, 6, CH, 128), BF16),
            pltpu.VMEM((6, CIN, 128), BF16),
            pltpu.VMEM((2, CIN, 128), F32),
            pltpu.VMEM((NC, 8, 128), jnp.int32),
            pltpu.VMEM((NC, 4, CH, CW), BF16),
            pltpu.VMEM((NB, 4, CH, CW), BF16),
            pltpu.VMEM((4, 256, CW), BF16),
            pltpu.VMEM((512, 256), BF16),
            pltpu.VMEM((FR, CH, CW), BF16),
            pltpu.VMEM((K, 4, CH, CW), F32),
            pltpu.VMEM((NB, 4, CH, CW), BF16),
            pltpu.VMEM((2 * NC, 4, CH, CW), BF16),
            pltpu.VMEM((4, 128, 256), F32),
            pltpu.VMEM((4, 128, 256), F32),
            pltpu.VMEM((NC, 3, 8, 256), F32),
            pltpu.VMEM((NC, 3, 8, 256), F32),
            pltpu.VMEM((NR, 3, 8, 256), F32),
            pltpu.VMEM((NC, 3, 8, 256), F32),
            dma((4, 8)),
            dma((4, 8)),
            dma((NC,)),
            dma((NC,)),
            dma((NC,)),
            dma((NB,)),
            dma((NC,)),
            dma((NC + 4,)),
            dma((2 * NC,)),
            dma((NC,)),
            dma((NC,)),
            dma((NR,)),
            dma((NR,)),
            dma((NC,)),
            dma((NC,)),
        ],
        compiler_params=pltpu.CompilerParams(
            collective_id=0, has_side_effects=True, vmem_limit_bytes=56 * 1024 * 1024
        ),
        cost_estimate=pl.CostEstimate(flops=4_000_000_000, bytes_accessed=8_000_000, transcendentals=524_288),
    )(
        block_ids,
        weight_ids,
        col_start,
        coarse,
        noisy,
        cotangent,
        rowsx,
        interp_cols,
        pair_matrix(first_weight),
        pair_matrix(second_weight),
        pair_matrix(adjoint(first_weight[:, :, :, FS:])),
        pair_matrix(adjoint(second_weight)),
    )


def solution(mesh):
    in_specs = (
        P(("row", "col"), None, None),
        P(None, "row", "col"),
        P(None, "row", "col"),
        P(),
        P(),
        P(),
        P(),
        P(("row", "col"), None),
        P(("row", "col"), None),
        P("col"),
    )
    out_specs = (P(None, "row", "col"), P(), P(), P(("row", "col"), None, None))
    return jax.shard_map(local, mesh=mesh, in_specs=in_specs, out_specs=out_specs, check_vma=False)
```

time: 529 us -> 135 us (0.26); the launches traced: 520 us -> 133 us
  waiting for transfers between devices: 192 us -> 0 us
  local copies, waits for them, and re-layouts: 155 us -> 8.75 us
  Pallas kernels: 0 us -> 120 us
  matrix products: 65.3 us -> 0 us
  starting transfers between devices: 57 us -> 0 us
  other arithmetic: 27.5 us -> 2.44 us
  between operations: 23.8 us -> 1.36 us
    pallas_call x0 -> x1, Pallas kernels: none -> 120 us  [local(): pl.pallas_call(kernel, out_shape=(jax.ShapeDtypeStruct((CH, FR, 256), BF1...]
    psum x1 -> x0, waiting for transfers between devices: 113 us -> none  [local(): lax.psum((first_local, second_local), ('row', 'col'))]
    reduce_scatter x1 -> x0, waiting for transfers between devices: 76.7 us -> none  [local(): lax.psum_scatter(spread, 'col', scatter_dimension=0, tiled=True)]
    dot_general x57 -> x0, matrix products: 65.3 us -> none  [the longest x18 30.9 us: weight_grad(): lax.dot_general(flat, shifted(padded, row_off, col_off, tile_rows, tile_c...]
    ppermute x20 -> x0, starting transfers between devices: 56.9 us -> none  [the longest x9 36.1 us: with_halo(): lax.ppermute(tail, axis, [(i, (i + 1) % count) for i in range(ends)])]
    slice x24 -> x1, local copies, waits for them, and re-layouts: 55.9 us -> 0.11 us  [local(): first_weight[:, :, :, FS:]]
    unnamed x125 -> x14, local copies, waits for them, and re-layouts: 58.8 us -> 5.95 us
    concatenate x11 -> x3, other arithmetic: 21.2 us -> 2.44 us  [pair_matrix(): jnp.concatenate([jnp.concatenate([flat, none], axis=1), jnp.concatenate([...]
  transfers between devices with their start and end apart: 23 -> 0, of which waited for: 3 -> 0; matrix products, arithmetic and copies ran while one was open for 31% -> 0% of each run, Pallas kernels for 0% -> 0%
where the time goes in v1:
time: 135 us; the launch traced here: 133 us
  Pallas kernels  120 us (89%)
  local copies, waits for them, and re-layouts  8.75 us (6%)
  other arithmetic  2.44 us (2%)
  between operations  1.36 us (1%)
    pallas_call x1, Pallas kernels, local(): pl.pallas_call(kernel, out_shape=(jax.ShapeDtypeStruct((CH, FR, 256), BF1...  120 us
    unnamed x14, local copies, waits for them, and re-layouts  5.95 us

profile of v1, /device:TPU:1, one launch (start us, length us, event | category | flops | bytes accessed | tf_op | source)
XLA Modules:
  0.0 132.9 jit_solution(9656264609102468455)
XLA Ops:
  1.3 0.0 copy-start
  1.3 0.8 broadcast_in_dim.4
  2.0 0.1 copy.19
  2.2 0.0 copy-done
  2.2 0.1 copy.21
  2.4 0.0 copy-start.1
  2.4 0.1 copy.22
  2.5 0.8 copy-done.1
  3.3 0.1 slice.3
  3.4 0.1 copy.24
  3.6 0.1 copy.26
  3.7 0.8 fusion.11.wb2
  4.5 0.1 tile.11
  4.6 0.9 tile.12.rowsx
  5.4 0.1 copy.20
  5.6 0.2 reshape.24
  5.7 0.8 fusion.8.wf1
  6.5 0.9 fusion.9
  7.4 120.4 %shard_map.129 = (bf16[64,32,256]{2,1,0:T(8,128)(2,1)}, f32[3,3,64,80]{3,2,1,0:T(8,128)}, f32[3,3,64,64]{3,2,1,0:T(8,128)}, f32[4,64,256]{2,1,0:T(8,128)}) custom-call(s32[1,4]{1,0:T(1,128)} %block_ids.1, s32[1,4]{1,0:T(1,128)} %weight_ids.1, s32[1]{0:T(128)S(6)} %copy.32.col_start, bf16[4,64,256]{2,1,0:T(8,128)(2,1)} %coarse.1, bf16[16,32,256]{2,1,0:T(8,128)(2,1)} %noisy.1, ...), custom_call_target="tpu_custom_call" | custom-call | flops 4000000000 | bytes 8000000 | tf_op jit(solution)/shard_map/pallas_call | solution.py:554
  127.8 0.0 copy-start.3
  127.8 2.3 %copy.33 = bf16[64,32,256]{2,1,0:T(8,128)(2,1)} copy(bf16[64,32,256]{2,1,0:T(8,128)(2,1)} %get-tuple-element.10) | data formatting | bytes 2097152
  130.1 0.0 copy-done.3
  130.1 0.0 copy-start.2
  130.1 0.7 copy.34
  130.8 0.4 copy-done.2
  131.2 0.0 copy-start.4
  131.2 0.7 copy.35
  131.9 0.3 copy-done.4
  132.2 0.7 copy.36
  (2 shorter events, 0.0 us)
Async XLA Ops:
  1.3 0.9 copy-start
  2.4 0.9 copy-start.1
  127.8 2.3 %copy-start.3 = (f32[3,3,64,80]{3,2,1,0:T(8,128)S(1)}, f32[3,3,64,80]{3,2,1,0:T(8,128)}, u32[]{:S(2)}) copy-start(f32[3,3,64,80]{3,2,1,0:T(8,128)} %get-tuple-element.11) | copy-start | bytes 552964
  130.1 1.1 copy-start.2
  131.2 1.1 copy-start.4

commit v2 on v1

v2 whole, which is shorter than its diff:
```python
import jax
import jax.numpy as jnp
from jax import lax
from jax.experimental import pallas as pl
from jax.experimental.pallas import tpu as pltpu
from jax.sharding import PartitionSpec as P

F32 = jnp.float32
BF16 = jnp.bfloat16
MESH = pl.DeviceIdType.MESH

NR = 8
NC = 16
HB = 2
K = 4
FR = 32
CH = 64
FS = 16
CIN = 80
CW = 128
NB = NC + 2 * HB

DIRS = ((0, 1), (0, -1), (1, 1), (1, -1), (-1, 1), (-1, -1))
COT, INP, HID, ACT = range(4)


def iota(shape, dim):
    return lax.broadcasted_iota(jnp.int32, shape, dim)


def dot(a, b):
    return jnp.dot(a, b, preferred_element_type=F32)


def dot_nt(a, b):
    return lax.dot_general(a, b, (((1,), (1,)), ((), ())), preferred_element_type=F32)


def one_hot(hit):
    return jnp.where(hit, 1.0, 0.0).astype(BF16)


def permutation():
    i0, i1 = iota((256, 256), 0), iota((256, 256), 1)
    return one_hot((lax.rem(i0, 16) == lax.div(i1, 16)) & (lax.div(i0, 16) == lax.rem(i1, 16)))


def kernel(
    block_ids,
    weight_ids,
    col_start,
    coarse,
    noisy,
    cot,
    rows,
    cols,
    first_w,
    second_w,
    fine_hbm,
    grads_out,
    coarse_out,
    v_cot,
    v_in,
    v_hid,
    v_act,
    g_cot,
    g_act,
    hgrad,
    pre,
    fine,
    wf1,
    wf2,
    wb1,
    wb2,
    edge,
    edge_in,
    edge_got,
    edge_got_in,
    around,
    around_in,
    fix,
    cs,
    slab,
    gath,
    pieces,
    lmat,
    sec,
    pgrad,
    sbuf,
    rbuf,
    rhalo,
    spots,
    acc1,
    acc2,
    gbuf,
    gpart,
    grow,
    x_send,
    x_recv,
    cs_send,
    cs_recv,
    ag_send,
    ag_recv,
    rs_send,
    rs_recv,
    rh_send,
    rh_recv,
    w1_send,
    w1_recv,
    w2_send,
    w2_recv,
    w3_send,
    w3_recv,
    out_sem,
):
    r = lax.axis_index("row")
    c = lax.axis_index("col")
    lane = iota((CH, 128), 1)

    def row_at(d):
        return lax.rem(r + (d + NR), NR)

    def col_at(d):
        return lax.rem(c + (d + NC), NC)

    def remote(src, dst, send, recv, device):
        return pltpu.make_async_remote_copy(
            src_ref=src, dst_ref=dst, send_sem=send, recv_sem=recv, device_id=device, device_id_type=MESH
        )

    barrier = pltpu.get_barrier_semaphore()
    met = [(0, d) for d in range(1, NC)] + [(d, 0) for d in range(1, NR)]
    met += [(dr, dc) for dr in (-1, 1) for dc in (-1, 1)]
    for dr, dc in met:
        pl.semaphore_signal(barrier, inc=1, device_id=(row_at(dr), col_at(dc)), device_id_type=MESH)

    perm = permutation()

    def flip_in(src, dst, c0, h0):
        block = src[c0 : c0 + 16, h0 : h0 + 16, :].reshape(256, 256)
        dst[1 + h0 : 17 + h0, c0 : c0 + 16, :] = dot(perm, block).astype(BF16).reshape(16, 16, 256)

    for c0 in range(0, CH, 16):
        for h0 in range(0, FR, 16):
            flip_in(cot, v_cot, c0, h0)
    for h0 in range(0, FR, 16):
        flip_in(noisy, v_in, 0, h0)

    def place(ins, at):
        return one_hot(iota((ins, 256), 1) == iota((ins, 256), 0) + at)

    wf1[...] = sum(dot(first_w[a].reshape(3 * CH, CIN), place(CIN, a * CIN)) for a in range(3)).astype(BF16)
    for row in range(2):
        flat = sum(dot(second_w[a].reshape(3 * CH, CH), place(CH, (a + row) * CH)) for a in range(3))
        wf2[:, row] = flat.astype(BF16).reshape(3, CH, 256)
    for w, back, ins, skip in ((first_w, wb1, CIN, FS), (second_w, wb2, CH, 0)):
        pick = one_hot(iota((CH, ins), 1) == iota((CH, ins), 0) + skip)
        none = jnp.zeros((CH, ins), BF16)
        for e in range(3):
            taps = [w[2 - a, 2 - e] for a in range(3)]
            back[e, 0] = dot_nt(pick, jnp.concatenate(taps + [none], axis=0)).astype(BF16)
            back[e, 1] = dot_nt(pick, jnp.concatenate([none] + taps, axis=0)).astype(BF16)

    lane256 = iota((FR, 256), 1)
    repeat = one_hot(lax.rem(lax.div(iota((4, 256), 1), 16), 4) == iota((4, 256), 0))
    table = jnp.zeros((FR, 256), F32)
    for k in range(K):
        table = jnp.where(lax.div(lane256, 64) == k, dot(rows[weight_ids[0, k]], repeat), table)
    spread = one_hot(lax.div(iota((512, FR), 0), 16) == iota((512, FR), 1))
    same = lax.rem(iota((512, 256), 0), 16) == lax.rem(iota((512, 256), 1), 16)
    lmat[...] = jnp.where(same, dot(spread, table.astype(BF16)), 0.0).astype(BF16)

    def put_shifted(g, h, t0, t1, count):
        low = iota(t0.shape, 1) == 0
        high = iota(t0.shape, 1) == 127
        r0, r1 = pltpu.roll(t0, 1, 1), pltpu.roll(t1, 1, 1)
        s0, s1 = pltpu.roll(t0, 127, 1), pltpu.roll(t1, 127, 1)

        def put(e, half, value):
            g[pl.ds(h, count), e, :, 128 * half : 128 * half + 128] = value.astype(BF16).reshape(count, CH, 128)

        put(0, 0, jnp.where(high, s1, s0))
        put(0, 1, jnp.where(high, 0.0, s1))
        put(1, 0, t0)
        put(1, 1, t1)
        put(2, 0, jnp.where(low, 0.0, r0))
        put(2, 1, jnp.where(low, r0, r1))

    def shift_cot(h, _):
        put_shifted(g_cot, h, v_cot[h + 1, :, 0:128].astype(F32), v_cot[h + 1, :, 128:256].astype(F32), 1)
        return 0

    bufs = {
        COT: (v_cot, edge.at[0], edge_got.at[0], around.at[0], CH),
        INP: (v_in, edge_in, edge_got_in, around_in, CIN),
        HID: (v_hid, edge.at[1], edge_got.at[1], around.at[1], CH),
        ACT: (v_act, edge.at[2], edge_got.at[2], around.at[2], CH),
    }

    def halo_pack(x):
        v, e, _, _, chans = bufs[x]
        at = iota((chans, 128), 1)

        def pack(h, held):
            left = v[h + 1, :, 0:128].astype(F32)[:, 0:1]
            right = v[h + 1, :, 128:256].astype(F32)[:, 127:128]
            held = jnp.where(at == h, left, held)
            return jnp.where(at == h + 64, right, held)

        e[...] = lax.fori_loop(0, FR, pack, jnp.zeros((chans, 128), F32), unroll=4).astype(BF16)

    def halo_copies(x):
        v, e, got, _, _ = bufs[x]
        copies = [
            remote(e, got.at[i], x_send.at[x, i], x_recv.at[x, i], (row_at(dr), col_at(dc)))
            for i, (dr, dc) in enumerate(DIRS)
        ]
        copies.append(remote(v.at[FR], v.at[0], x_send.at[x, 6], x_recv.at[x, 6], (row_at(1), c)))
        copies.append(remote(v.at[1], v.at[FR + 1], x_send.at[x, 7], x_recv.at[x, 7], (row_at(-1), c)))
        return copies

    def halo_start(x):
        halo_pack(x)
        for copy in halo_copies(x):
            copy.start()

    def halo_finish(x):
        v, _, got, ring, chans = bufs[x]
        for copy in halo_copies(x):
            copy.wait()
        at = iota((chans, 128), 1)

        @pl.when(r == 0)
        def _():
            v[0] = jnp.zeros((chans, 256), BF16)

        @pl.when(r == NR - 1)
        def _():
            v[FR + 1] = jnp.zeros((chans, 256), BF16)

        top = (r > 0).astype(F32)
        bottom = (r < NR - 1).astype(F32)
        west = (c > 0).astype(F32)
        east = (c < NC - 1).astype(F32)

        def side(mid, up, down, first, there):
            a = pltpu.roll(got[mid].astype(F32), 65, 1)
            b = pltpu.roll(got[up].astype(F32), 33, 1) * top
            d = pltpu.roll(got[down].astype(F32), 97, 1) * bottom
            return jnp.where(at == first, b, jnp.where(at == first + FR + 1, d, a)) * there

        both = jnp.where(at < 64, side(0, 2, 4, 0, west), side(1, 3, 5, 64, east))
        ring[0] = both.astype(BF16)
        ring[1] = pltpu.roll(both, 127, 1).astype(BF16)
        ring[2] = pltpu.roll(both, 126, 1).astype(BF16)

    def combine(prod, n, low, high):
        at = iota((n, 128), 1)
        a0, a1 = prod[0:n, 0:128], prod[0:n, 128:256]
        b0, b1 = prod[n : 2 * n, 0:128], prod[n : 2 * n, 128:256]
        d0, d1 = prod[2 * n : 3 * n, 0:128], prod[2 * n : 3 * n, 128:256]
        r0, r1 = pltpu.roll(a0, 1, 1), pltpu.roll(a1, 1, 1)
        s0, s1 = pltpu.roll(d0, 127, 1), pltpu.roll(d1, 127, 1)
        t0 = b0 + jnp.where(at == 0, low, r0) + jnp.where(at == 127, s1, s0)
        t1 = b1 + jnp.where(at == 0, r0, r1) + jnp.where(at == 127, high, s1)
        return t0, t1

    def set_fix(x, left, right):
        ring, chans = bufs[x][3], bufs[x][4]
        cells = ring[...].reshape(3 * chans, 128)
        fix[...] = jnp.where(lane < 64, dot(left, cells), dot(right, cells))

    def fix_low(h):
        return pltpu.roll(fix[...], lax.rem(128 - h, 128), 1)

    def fix_high(h):
        return pltpu.roll(fix[...], 63 - h, 1)

    def set_pair_fix(x, weights):
        set_fix(x, weights[0, 0][:, 0 : 3 * CH], weights[2, 0][:, 0 : 3 * CH])

    def conv_pair(weights, v, p):
        prod = dot(weights[...].reshape(6 * CH, 256), v[pl.ds(2 * p, 4)].reshape(256, 256))
        low = jnp.concatenate([fix_low(2 * p), fix_low(2 * p + 1)], axis=0)
        high = jnp.concatenate([fix_high(2 * p), fix_high(2 * p + 1)], axis=0)
        return combine(prod, 2 * CH, low, high)

    halo_pack(COT)

    pl.semaphore_wait(barrier, len(met))

    cs[c] = jnp.full((8, 128), col_start[0], jnp.int32)

    def cs_copy(d):
        return remote(cs.at[c], cs.at[c], cs_send.at[d], cs_recv.at[c], (r, col_at(d)))

    def cs_arrival(d):
        other = col_at(d)
        return remote(cs.at[other], cs.at[other], cs_send.at[d], cs_recv.at[other], (r, other))

    for d in range(1, NC):
        cs_copy(d).start()
    for copy in halo_copies(COT):
        copy.start()
    lax.fori_loop(0, FR, shift_cot, 0, unroll=2)
    for d in range(1, NC):
        cs_copy(d).wait_send()
        cs_arrival(d).wait_recv()

    def ag_copy(d):
        to = col_at(d)
        return remote(slab.at[to], gath.at[HB + c], ag_send.at[d], ag_recv.at[HB + c], (r, to))

    whole = coarse[...].reshape(256, 256)

    def cut(d, _):
        to = col_at(d)
        start = cs[to][0:1, :]
        pick = one_hot(iota((256, 128), 0) == iota((256, 128), 1) + start)
        slab[to] = dot(whole, pick).astype(BF16).reshape(4, CH, CW)

        @pl.when(d > 0)
        def _():
            ag_copy(d).start()

        @pl.when(d == 0)
        def _():
            gath[HB + c] = slab[c]

        return 0

    lax.fori_loop(0, NC, cut, 0)

    def set_spot(n, _):
        start = cs[n][0:1, :]
        start = jnp.concatenate([start, start], axis=1)
        spots[n] = one_hot(iota((CW, 256), 1) == iota((CW, 256), 0) + start)
        return 0

    lax.fori_loop(0, NC, set_spot, 0)

    halo_finish(COT)
    set_pair_fix(COT, wb2)

    def hidden_grad(p, _):
        t0, t1 = conv_pair(wb2, v_cot, p)
        hgrad[pl.ds(2 * p, 2), :, 0:128] = t0.reshape(2, CH, 128)
        hgrad[pl.ds(2 * p, 2), :, 128:256] = t1.reshape(2, CH, 128)
        return 0

    lax.fori_loop(0, FR // 2, hidden_grad, 0, unroll=2)

    def ag_arrival(slot):
        return remote(slab.at[0], gath.at[slot], ag_send.at[0], ag_recv.at[slot], (r, col_at(1)))

    def pass_on(n):
        src, dst, dr = ((NC, 0, 1), (NC + 1, 1, 1), (HB, NC + HB, -1), (HB + 1, NC + HB + 1, -1))[n]
        return remote(gath.at[src], gath.at[dst], ag_send.at[NC + n], ag_recv.at[dst], (row_at(dr), c))

    for n, at in enumerate((NC - 2, NC - 1, 0, 1)):
        @pl.when(c != at)
        def _():
            ag_arrival(HB + at).wait_recv()

        pass_on(n).start()
    for at in range(2, NC - 2):
        @pl.when(c != at)
        def _():
            ag_arrival(HB + at).wait_recv()

    for d in range(1, NC):
        ag_copy(d).wait_send()
    for n in range(4):
        pass_on(n).wait()

    first_block = r * NC - HB
    for k in range(K):
        piece = gath[jnp.clip(block_ids[0, k] - first_block, 0, NB - 1)]
        for g in range(4):
            pieces[g, 64 * k : 64 * k + 64, :] = piece[:, 16 * g : 16 * g + 16, :].reshape(64, CW)
    for g in range(4):
        sec[:, 16 * g : 16 * g + 16, :] = dot(lmat[...], pieces[g]).astype(BF16).reshape(FR, 16, CW)

    def regrid(q, _):
        flat = sec[pl.ds(4 * q, 4)].reshape(256, CW)
        v_in[pl.ds(1 + 4 * q, 4), FS:CIN, :] = dot(flat, cols[...]).astype(BF16).reshape(4, CH, 256)
        return 0

    lax.fori_loop(0, FR // 4, regrid, 0, unroll=2)

    halo_start(INP)

    def first_row(h, _):
        prod = dot(wf1[:, 0 : 3 * CIN], v_in[pl.ds(h, 3)].reshape(3 * CIN, 256))
        t0, t1 = combine(prod, CH, 0.0, 0.0)
        pre[h, :, 0:128] = t0
        pre[h, :, 128:256] = t1
        return 0

    lax.fori_loop(1, FR - 1, first_row, 0, unroll=2)

    halo_finish(INP)
    first_row(0, 0)
    first_row(FR - 1, 0)
    set_fix(INP, wf1[0:CH, 0 : 3 * CIN], wf1[2 * CH : 3 * CH, 0 : 3 * CIN])

    def activate(h, _):
        t0 = pre[h, :, 0:128] + jnp.where(lane == 0, fix_low(h), 0.0)
        t1 = pre[h, :, 128:256] + jnp.where(lane == 127, fix_high(h), 0.0)
        back = []
        for half, t in ((0, t0), (1, t1)):
            at = slice(128 * half, 128 * half + 128)
            s = 1.0 / (1.0 + jnp.exp(-t))
            v_hid[h + 1, :, at] = (t * s).astype(BF16)
            grad = hgrad[h, :, at] * (s * (1.0 + t * (1.0 - s)))
            v_act[h + 1, :, at] = grad.astype(BF16)
            back.append(grad)
        put_shifted(g_act, h, back[0], back[1], 1)
        return 0

    lax.fori_loop(0, FR, activate, 0, unroll=2)
    halo_start(HID)
    halo_start(ACT)

    edges = ((jnp.where(lane < 64, 1.0, 0.0)).astype(BF16), (jnp.where(lane < 64, 0.0, 1.0)).astype(BF16))

    def edge_terms(x, of):
        ring, chans = bufs[x][3], bufs[x][4]
        mine = bufs[of][1][...]
        both = jnp.concatenate([mine * edges[0], mine * edges[1]], axis=0)
        return dot_nt(both, ring[...].reshape(3 * chans, 128))

    acc1[...] = jnp.zeros(acc1.shape, F32)

    def first_grad(h, _):
        acc1[:, 0 : 3 * CIN] += dot_nt(g_act[h].reshape(3 * CH, 256), v_in[pl.ds(h, 3)].reshape(3 * CIN, 256))
        return 0

    lax.fori_loop(0, FR, first_grad, 0, unroll=2)
    extra = edge_terms(INP, ACT)
    acc1[0:CH, 0 : 3 * CIN] += extra[0:CH]
    acc1[2 * CH :, 0 : 3 * CIN] += extra[CH:]
    gbuf[0:8] = acc1[...].reshape(8, 24, 256)

    halo_finish(HID)
    acc2[...] = jnp.zeros(acc2.shape, F32)

    def second_grad(p, _):
        acc2[...] += dot_nt(g_cot[pl.ds(2 * p, 2)].reshape(6 * CH, 256), v_hid[pl.ds(2 * p, 4)].reshape(256, 256))
        return 0

    lax.fori_loop(0, FR // 2, second_grad, 0, unroll=2)
    extra = edge_terms(HID, COT)
    acc2[0 : 3 * CH, :] += pltpu.roll(acc2[3 * CH :, :], 192, 1)
    acc2[0:CH, 0 : 3 * CH] += extra[0:CH]
    acc2[2 * CH : 3 * CH, 0 : 3 * CH] += extra[CH:]
    gbuf[8:16] = acc2[0 : 3 * CH, :].reshape(8, 24, 256)

    def w1_copy(d):
        to = col_at(d)
        return remote(gbuf.at[to], gpart.at[c], w1_send.at[d], w1_recv.at[c], (r, to))

    for d in range(1, NC):
        w1_copy(d).start()
    gpart[c] = gbuf[c]

    halo_finish(ACT)
    set_pair_fix(ACT, wb1)

    def cond_grad(p, _):
        t0, t1 = conv_pair(wb1, v_act, p)
        fine[pl.ds(2 * p, 2), :, 0:128] = t0.astype(BF16).reshape(2, CH, 128)
        fine[pl.ds(2 * p, 2), :, 128:256] = t1.astype(BF16).reshape(2, CH, 128)
        return 0

    lax.fori_loop(0, FR // 2, cond_grad, 0, unroll=2)

    def section_grad(q, _):
        flat = fine[pl.ds(8 * q, 8)].reshape(512, 256)
        sec[pl.ds(8 * q, 8)] = dot_nt(flat, cols[...]).astype(BF16).reshape(8, CH, CW)
        return 0

    lax.fori_loop(0, FR // 8, section_grad, 0)
    eye = one_hot(iota((256, 256), 0) == iota((256, 256), 1))
    lmat_t = dot_nt(eye, lmat[...]).astype(BF16)
    for g in range(4):
        part = dot(lmat_t, sec[:, 16 * g : 16 * g + 16, :].reshape(512, CW))
        pgrad[:, :, 16 * g : 16 * g + 16, :] = part.reshape(K, 4, 16, CW)

    def contribution(b):
        total = None
        for k in range(K):
            hit = (block_ids[0, k] - first_block == b).astype(F32)
            term = pgrad[k] * hit
            total = term if total is None else total + term
        return total

    def rh_copy(n):
        b, dr = ((0, -1), (1, -1), (NB - 2, 1), (NB - 1, 1))[n]
        return remote(sbuf.at[b], rhalo.at[n], rh_send.at[n], rh_recv.at[n], (row_at(dr), c))

    for n, b in enumerate((0, 1, NB - 2, NB - 1)):
        sbuf[b] = contribution(b).astype(BF16)
        rh_copy(n).start()

    def rs_copy(to):
        return remote(sbuf.at[HB + to], rbuf.at[c], rs_send.at[to], rs_recv.at[c], (r, to))

    def send_block(to):
        @pl.when(to != c)
        def _():
            rs_copy(to).start()

        @pl.when(to == c)
        def _():
            rbuf[c] = sbuf[HB + to]

    def inner(n, _):
        to = 2 + lax.rem(c + n, NC - 4)
        sbuf[HB + to] = contribution(HB + to).astype(BF16)
        send_block(to)
        return 0

    lax.fori_loop(0, 8, inner, 0)
    for n in range(4):
        rh_copy(n).wait()

    def outer(n, _):
        i = lax.rem(n + c, 4)
        to = lax.rem(NC - 2 + i, NC)
        sbuf[HB + to] = (contribution(HB + to) + rhalo[i].astype(F32)).astype(BF16)
        send_block(to)
        inner(8 + n, 0)
        return 0

    lax.fori_loop(0, 4, outer, 0)

    for d in range(1, NC):
        w1_copy(d).wait_send()
        other = col_at(d)
        remote(gbuf.at[other], gpart.at[other], w1_send.at[d], w1_recv.at[other], (r, other)).wait_recv()
    total = gpart[0]
    for n in range(1, NC):
        total = total + gpart[n]
    grow[r] = total

    def w2_copy(d):
        return remote(grow.at[r], grow.at[r], w2_send.at[d], w2_recv.at[r], (row_at(d), c))

    for d in range(1, NR):
        w2_copy(d).start()

    set_pair_fix(HID, wf2)

    def second_level(p, _):
        t0, t1 = conv_pair(wf2, v_hid, p)
        fine[pl.ds(2 * p, 2), :, 0:128] = t0.astype(BF16).reshape(2, CH, 128)
        fine[pl.ds(2 * p, 2), :, 128:256] = t1.astype(BF16).reshape(2, CH, 128)
        return 0

    lax.fori_loop(0, FR // 4, second_level, 0, unroll=2)

    for d in range(1, NR):
        w2_copy(d).wait_send()
        other = row_at(d)
        remote(grow.at[other], grow.at[other], w2_send.at[d], w2_recv.at[other], (other, c)).wait_recv()
    total = grow[0]
    for n in range(1, NR):
        total = total + grow[n]
    grads_out[c] = total

    def w3_copy(d):
        return remote(grads_out.at[c], grads_out.at[c], w3_send.at[d], w3_recv.at[c], (r, col_at(d)))

    for d in range(1, NC):
        w3_copy(d).start()

    lax.fori_loop(FR // 4, FR // 2, second_level, 0, unroll=2)
    out = pltpu.make_async_copy(fine, fine_hbm, out_sem)
    out.start()

    for n in range(NC):
        @pl.when(n != c)
        def _():
            rs_copy(n).wait_send()
            remote(sbuf.at[0], rbuf.at[n], rs_send.at[n], rs_recv.at[n], (r, n)).wait_recv()

    def add(q, _):
        flat = [rbuf[4 * q + n].reshape(256, CW) for n in range(4)]
        spot = spots[pl.ds(4 * q, 4)].reshape(4 * CW, 256)
        coarse_out[...] += dot(jnp.concatenate(flat, axis=1), spot).reshape(4, CH, 256)
        return 0

    coarse_out[...] = jnp.zeros((4, CH, 256), F32)
    lax.fori_loop(0, NC // 4, add, 0)

    for d in range(1, NC):
        w3_copy(d).wait_send()
        other = col_at(d)
        remote(grads_out.at[other], grads_out.at[other], w3_send.at[d], w3_recv.at[other], (r, other)).wait_recv()
    out.wait()


def results(fine, grads, block, fine_out, first_out, second_out, coarse_out):
    perm = permutation()
    for h0 in range(0, FR, 16):
        rows = fine[h0 : h0 + 16].reshape(256, 256)
        fine_out[:, h0 : h0 + 16, :] = dot(perm, rows).astype(BF16).reshape(16, 16, 256)

    @pl.when(pl.program_id(0) == 0)
    def _():
        coarse_out[...] = block[...]
        first = grads[0:8].reshape(3 * CH, 256)
        second = grads[8:16].reshape(3 * CH, 256)
        for a in range(3):
            for e in range(3):
                first_out[a, e] = first[e * CH : (e + 1) * CH, a * CIN : (a + 1) * CIN]
                second_out[a, e] = second[e * CH : (e + 1) * CH, a * CH : (a + 1) * CH]


def local(
    coarse,
    noisy,
    cotangent,
    interp_rows,
    interp_cols,
    first_weight,
    second_weight,
    block_ids,
    weight_ids,
    col_start,
):
    smem = pl.BlockSpec(memory_space=pltpu.SMEM)
    vmem = pl.BlockSpec(memory_space=pltpu.VMEM)
    dma = pltpu.SemaphoreType.DMA
    fine, grads, block = pl.pallas_call(
        kernel,
        out_shape=(
            jax.ShapeDtypeStruct((FR, CH, 256), BF16),
            jax.ShapeDtypeStruct((NC, 24, 256), F32),
            jax.ShapeDtypeStruct((4, CH, 256), F32),
        ),
        in_specs=[smem] * 3 + [vmem] * 7,
        out_specs=(pl.BlockSpec(memory_space=pl.ANY), vmem, vmem),
        scratch_shapes=[
            pltpu.VMEM((FR + 2, CH, 256), BF16),
            pltpu.VMEM((FR + 2, CIN, 256), BF16),
            pltpu.VMEM((FR + 2, CH, 256), BF16),
            pltpu.VMEM((FR + 2, CH, 256), BF16),
            pltpu.VMEM((FR, 3, CH, 256), BF16),
            pltpu.VMEM((FR, 3, CH, 256), BF16),
            pltpu.VMEM((FR, CH, 256), F32),
            pltpu.VMEM((FR, CH, 256), F32),
            pltpu.VMEM((FR, CH, 256), BF16),
            pltpu.VMEM((3 * CH, 256), BF16),
            pltpu.VMEM((3, 2, CH, 256), BF16),
            pltpu.VMEM((3, 2, CH, 256), BF16),
            pltpu.VMEM((3, 2, CH, 256), BF16),
            pltpu.VMEM((3, CH, 128), BF16),
            pltpu.VMEM((CIN, 128), BF16),
            pltpu.VMEM((3, 6, CH, 128), BF16),
            pltpu.VMEM((6, CIN, 128), BF16),
            pltpu.VMEM((3, 3, CH, 128), BF16),
            pltpu.VMEM((3, CIN, 128), BF16),
            pltpu.VMEM((CH, 128), F32),
            pltpu.VMEM((NC, 8, 128), jnp.int32),
            pltpu.VMEM((NC, 4, CH, CW), BF16),
            pltpu.VMEM((NB, 4, CH, CW), BF16),
            pltpu.VMEM((4, 256, CW), BF16),
            pltpu.VMEM((512, 256), BF16),
            pltpu.VMEM((FR, CH, CW), BF16),
            pltpu.VMEM((K, 4, CH, CW), F32),
            pltpu.VMEM((NB, 4, CH, CW), BF16),
            pltpu.VMEM((NC, 4, CH, CW), BF16),
            pltpu.VMEM((4, 4, CH, CW), BF16),
            pltpu.VMEM((NC, CW, 256), BF16),
            pltpu.VMEM((3 * CH, 256), F32),
            pltpu.VMEM((6 * CH, 256), F32),
            pltpu.VMEM((NC, 24, 256), F32),
            pltpu.VMEM((NC, 24, 256), F32),
            pltpu.VMEM((NR, 24, 256), F32),
            dma((4, 8)),
            dma((4, 8)),
            dma((NC,)),
            dma((NC,)),
            dma((NC + 4,)),
            dma((NB,)),
            dma((NC,)),
            dma((NC,)),
            dma((4,)),
            dma((4,)),
            dma((NC,)),
            dma((NC,)),
            dma((NR,)),
            dma((NR,)),
            dma((NC,)),
            dma((NC,)),
            dma,
        ],
        compiler_params=pltpu.CompilerParams(
            collective_id=0, has_side_effects=True, vmem_limit_bytes=56 * 1024 * 1024
        ),
        cost_estimate=pl.CostEstimate(flops=4_000_000_000, bytes_accessed=8_000_000, transcendentals=524_288),
    )(
        block_ids,
        weight_ids,
        col_start,
        coarse,
        noisy,
        cotangent,
        interp_rows,
        interp_cols,
        first_weight,
        second_weight,
    )
    whole = lambda *shape: pl.BlockSpec(shape, lambda g: (0,) * len(shape))
    return pl.pallas_call(
        results,
        grid=(CH // 16,),
        out_shape=(
            jax.ShapeDtypeStruct((CH, FR, 256), BF16),
            jax.ShapeDtypeStruct((3, 3, CH, CIN), F32),
            jax.ShapeDtypeStruct((3, 3, CH, CH), F32),
            jax.ShapeDtypeStruct((4, CH, 256), F32),
        ),
        in_specs=[
            pl.BlockSpec((FR, 16, 256), lambda g: (0, g, 0)),
            whole(NC, 24, 256),
            whole(4, CH, 256),
        ],
        out_specs=(
            pl.BlockSpec((16, FR, 256), lambda g: (g, 0, 0)),
            whole(3, 3, CH, CIN),
            whole(3, 3, CH, CH),
            whole(4, CH, 256),
        ),
        compiler_params=pltpu.CompilerParams(vmem_limit_bytes=32 * 1024 * 1024),
        cost_estimate=pl.CostEstimate(flops=270_000_000, bytes_accessed=4_000_000, transcendentals=0),
    )(fine, grads, block)


def solution(mesh):
    in_specs = (
        P(("row", "col"), None, None),
        P(None, "row", "col"),
        P(None, "row", "col"),
        P(),
        P(),
        P(),
        P(),
        P(("row", "col"), None),
        P(("row", "col"), None),
        P("col"),
    )
    out_specs = (P(None, "row", "col"), P(), P(), P(("row", "col"), None, None))
    return jax.shard_map(local, mesh=mesh, in_specs=in_specs, out_specs=out_specs, check_vma=False)
```

time: 135 us -> 91.3 us (0.68); the launches traced: 133 us -> 90.8 us
  Pallas kernels: 120 us -> 84.9 us
  local copies, waits for them, and re-layouts: 8.75 us -> 4.62 us
  other arithmetic: 2.44 us -> 0 us
    pallas_call x1 -> x2, Pallas kernels: 120 us -> 84.9 us  [the longest x1 82.3 us: local(): pl.pallas_call(kernel, out_shape=(jax.ShapeDtypeStruct((FR, CH, 256), BF1...]
    concatenate x3 -> x0, other arithmetic: 2.44 us -> none  [pair_matrix(): jnp.concatenate([jnp.concatenate([flat, none], axis=1), jnp.concatenate([...]
    unnamed x14 -> x7, local copies, waits for them, and re-layouts: 5.95 us -> 4.62 us
where the time goes in v2:
time: 91.3 us; the launch traced here: 90.8 us
  Pallas kernels  84.9 us (93%)
  local copies, waits for them, and re-layouts  4.62 us (5%)
  between operations  1.3 us (1%)
    pallas_call x1, Pallas kernels, local(): pl.pallas_call(kernel, out_shape=(jax.ShapeDtypeStruct((FR, CH, 256), BF1...  82.3 us
    unnamed x7, local copies, waits for them, and re-layouts  4.62 us
    pallas_call x1, Pallas kernels, local(): pl.pallas_call(results, grid=(CH // 16,), out_shape=(jax.ShapeDtypeStruct...  2.63 us

profile of v2, /device:TPU:1, one launch (start us, length us, event | category | flops | bytes accessed | tf_op | source)
XLA Modules:
  0.0 90.8 jit_solution(17439037281311032519)
XLA Ops:
  1.3 1.5 %copy.14.rows = bf16[8,32,4]{2,1,0:T(8,128)(2,1)} copy(bf16[8,32,4]{1,2,0:T(4,128)(2,1)} %param.13) | data formatting | bytes 4096 | tf_op args[3]
  2.7 82.3 %shard_map.129 = (bf16[32,64,256]{2,1,0:T(8,128)(2,1)}, f32[16,24,256]{2,1,0:T(8,128)}, f32[4,64,256]{2,1,0:T(8,128)}) custom-call(s32[1,4]{1,0:T(1,128)} %block_ids.1, s32[1,4]{1,0:T(1,128)} %weight_ids.1, s32[1]{0:T(128)S(6)} %copy.15.col_start, bf16[4,64,256]{2,1,0:T(8,128)(2,1)} %coarse.1, bf16[16,32,256]{2,1,0:T(8,128)(2,1)} %noisy.1, ...), custom_call_target="tpu_custom_call" | custom-call | flops 4000000000 | bytes 8000000 | tf_op jit(solution)/shard_map/pallas_call | solution.py:636
  85.0 0.0 copy-start
  85.0 1.2 %copy-done = bf16[32,64,256]{2,1,0:T(8,128)(2,1)S(1)} copy-done((bf16[32,64,256]{2,1,0:T(8,128)(2,1)S(1)}, bf16[32,64,256]{2,1,0:T(8,128)(2,1)}, u32[]{:S(2)}) %copy-start) | copy-done | bytes 1048600
  86.2 0.0 copy-start.1
  86.2 1.0 %copy-done.1 = f32[16,24,256]{2,1,0:T(8,128)S(1)} copy-done((f32[16,24,256]{2,1,0:T(8,128)S(1)}, f32[16,24,256]{2,1,0:T(8,128)}, u32[]{:S(2)}) %copy-start.1) | copy-done | bytes 393240
  87.2 0.0 copy-start.2
  87.2 0.9 %copy-done.2 = f32[4,64,256]{2,1,0:T(8,128)S(1)} copy-done((f32[4,64,256]{2,1,0:T(8,128)S(1)}, f32[4,64,256]{2,1,0:T(8,128)}, u32[]{:S(2)}) %copy-start.2) | copy-done | bytes 262168
  88.2 2.6 %shard_map.130 = (bf16[64,32,256]{2,1,0:T(8,128)(2,1)}, f32[3,3,64,80]{3,2,1,0:T(8,128)}, f32[3,3,64,64]{3,2,1,0:T(8,128)}, f32[4,64,256]{2,1,0:T(8,128)}) custom-call(bf16[32,64,256]{2,1,0:T(8,128)(2,1)S(1)} %copy-done, f32[16,24,256]{2,1,0:T(8,128)S(1)} %copy-done.1, f32[4,64,256]{2,1,0:T(8,128)S(1)} %copy-done.2), custom_call_target="tpu_custom_call" | custom-call | flops 270000000 | bytes 4000000 | tf_op jit(solution)/shard_map/pallas_call | solution.py:717
Async XLA Ops:
  85.0 1.2 %copy-start = (bf16[32,64,256]{2,1,0:T(8,128)(2,1)S(1)}, bf16[32,64,256]{2,1,0:T(8,128)(2,1)}, u32[]{:S(2)}) copy-start(bf16[32,64,256]{2,1,0:T(8,128)(2,1)} %get-tuple-element.7.fine) | copy-start | bytes 3145732
  86.2 1.0 %copy-start.1 = (f32[16,24,256]{2,1,0:T(8,128)S(1)}, f32[16,24,256]{2,1,0:T(8,128)}, u32[]{:S(2)}) copy-start(f32[16,24,256]{2,1,0:T(8,128)} %get-tuple-element.8.grads) | copy-start | bytes 1179652
  87.2 0.9 %copy-start.2 = (f32[4,64,256]{2,1,0:T(8,128)S(1)}, f32[4,64,256]{2,1,0:T(8,128)}, u32[]{:S(2)}) copy-start(f32[4,64,256]{2,1,0:T(8,128)} %get-tuple-element.9.block) | copy-start | bytes 786436

commit v3 on v2

v3 whole, which is shorter than its diff:
```python
import jax
import jax.numpy as jnp
from jax import lax
from jax.experimental import pallas as pl
from jax.experimental.pallas import tpu as pltpu
from jax.sharding import PartitionSpec as P

F32 = jnp.float32
BF16 = jnp.bfloat16
MESH = pl.DeviceIdType.MESH

NR = 8
NC = 16
HB = 2
K = 4
FR = 32
CH = 64
FS = 16
CIN = 80
CW = 128
NB = NC + 2 * HB

PEERS = (
    ((2, 2), (1, 2), (2, 1), (3, 2), (2, 3), (1, 1), (3, 3), (1, 3))
    + ((3, 1), (0, 2), (2, 0), (0, 1), (1, 0), (0, 3), (3, 0))
)
COT, INP, HID, ACT = range(4)


def iota(shape, dim):
    return lax.broadcasted_iota(jnp.int32, shape, dim)


def dot(a, b):
    return jnp.dot(a, b, preferred_element_type=F32)


def dot_nt(a, b):
    return lax.dot_general(a, b, (((1,), (1,)), ((), ())), preferred_element_type=F32)


def dot_tn(a, b):
    return lax.dot_general(a, b, (((0,), (0,)), ((), ())), preferred_element_type=F32)


def one_hot(hit):
    return jnp.where(hit, 1.0, 0.0).astype(BF16)


def permutation():
    i0, i1 = iota((256, 256), 0), iota((256, 256), 1)
    return one_hot((lax.rem(i0, 16) == lax.div(i1, 16)) & (lax.div(i0, 16) == lax.rem(i1, 16)))


def kernel(
    block_ids,
    weight_ids,
    col_start,
    *rest,
):
    hbm, rest = rest[:7], rest[7:]
    body(block_ids, weight_ids, col_start, hbm, *rest)


def body(
    block_ids,
    weight_ids,
    col_start,
    hbm,
    fine_hbm,
    grads_out,
    coarse_out,
    coarse,
    noisy,
    cot,
    rows,
    cols,
    first_w,
    second_w,
    v_cot,
    v_in,
    v_hid,
    v_act,
    g_cot,
    g_act,
    hgrad,
    pre,
    fine,
    wf1,
    wf2,
    wb1,
    wb2,
    edge,
    edge_in,
    edge_got,
    edge_got_in,
    around,
    around_in,
    fix,
    cs,
    slab,
    gath,
    pieces,
    lmat,
    sec,
    pgrad,
    sbuf,
    rbuf,
    rhalo,
    spots,
    acc1,
    acc2,
    gbuf,
    gpart,
    grow,
    x_send,
    x_recv,
    cs_send,
    cs_recv,
    ag_send,
    ag_recv,
    rs_send,
    rs_recv,
    rh_send,
    rh_recv,
    w1_send,
    w1_recv,
    w2_send,
    w2_recv,
    w3_send,
    w3_recv,
    out_sem,
    in_sem,
):
    r = lax.axis_index("row")
    c = lax.axis_index("col")
    lane = iota((CH, 128), 1)

    def row_at(d):
        return lax.rem(r + (d + NR), NR)

    def col_at(d):
        return lax.rem(c + (d + NC), NC)

    def peer(n):
        dx, dy = PEERS[n]
        return lax.rem(lax.div(c, 4) + dx, 4) * 4 + lax.rem(c + dy, 4)

    def source(n):
        dx, dy = PEERS[n]
        return lax.rem(lax.div(c, 4) + 4 - dx, 4) * 4 + lax.rem(c + 4 - dy, 4)

    def remote(src, dst, send, recv, device):
        return pltpu.make_async_remote_copy(
            src_ref=src, dst_ref=dst, send_sem=send, recv_sem=recv, device_id=device, device_id_type=MESH
        )

    barrier = pltpu.get_barrier_semaphore()
    met = [(0, d) for d in range(1, NC)] + [(d, 0) for d in range(1, NR)]
    for dr, dc in met:
        pl.semaphore_signal(barrier, inc=1, device_id=(row_at(dr), col_at(dc)), device_id_type=MESH)

    fetched = [
        pltpu.make_async_copy(src, dst, in_sem.at[n])
        for n, (src, dst) in enumerate(zip(hbm, (coarse, noisy, cot, rows, cols, first_w, second_w)))
    ]
    for n in (2, 1, 5, 6, 3, 0, 4):
        fetched[n].start()
    for copy in fetched:
        copy.wait()
    perm = permutation()

    def flip_in(src, dst, c0, h0):
        block = src[c0 : c0 + 16, h0 : h0 + 16, :].reshape(256, 256)
        dst[1 + h0 : 17 + h0, c0 : c0 + 16, :] = dot(perm, block).astype(BF16).reshape(16, 16, 256)

    for c0 in range(0, CH, 16):
        for h0 in range(0, FR, 16):
            flip_in(cot, v_cot, c0, h0)
    for h0 in range(0, FR, 16):
        flip_in(noisy, v_in, 0, h0)

    def place(ins, at):
        return one_hot(iota((ins, 256), 1) == iota((ins, 256), 0) + at)

    wf1[...] = sum(dot(first_w[a].reshape(3 * CH, CIN), place(CIN, a * CIN)) for a in range(3)).astype(BF16)
    for row in range(2):
        flat = sum(dot(second_w[a].reshape(3 * CH, CH), place(CH, (a + row) * CH)) for a in range(3))
        wf2[:, row] = flat.astype(BF16).reshape(3, CH, 256)
    for w, back, ins, skip in ((first_w, wb1, CIN, FS), (second_w, wb2, CH, 0)):
        pick = one_hot(iota((CH, ins), 1) == iota((CH, ins), 0) + skip)
        none = jnp.zeros((CH, ins), BF16)
        for e in range(3):
            taps = [w[2 - a, 2 - e] for a in range(3)]
            back[e, 0] = dot_nt(pick, jnp.concatenate(taps + [none], axis=0)).astype(BF16)
            back[e, 1] = dot_nt(pick, jnp.concatenate([none] + taps, axis=0)).astype(BF16)

    lane256 = iota((FR, 256), 1)
    repeat = one_hot(lax.rem(lax.div(iota((4, 256), 1), 16), 4) == iota((4, 256), 0))
    table = jnp.zeros((FR, 256), F32)
    for k in range(K):
        table = jnp.where(lax.div(lane256, 64) == k, dot_tn(rows[weight_ids[0, k]], repeat), table)
    spread = one_hot(lax.div(iota((512, FR), 0), 16) == iota((512, FR), 1))
    same = lax.rem(iota((512, 256), 0), 16) == lax.rem(iota((512, 256), 1), 16)
    lmat[...] = jnp.where(same, dot(spread, table.astype(BF16)), 0.0).astype(BF16)

    def put_shifted(g, h, t0, t1, count):
        low = iota(t0.shape, 1) == 0
        high = iota(t0.shape, 1) == 127
        r0, r1 = pltpu.roll(t0, 1, 1), pltpu.roll(t1, 1, 1)
        s0, s1 = pltpu.roll(t0, 127, 1), pltpu.roll(t1, 127, 1)

        def put(e, half, value):
            g[pl.ds(h, count), e, :, 128 * half : 128 * half + 128] = value.astype(BF16).reshape(count, CH, 128)

        put(0, 0, jnp.where(high, s1, s0))
        put(0, 1, jnp.where(high, 0.0, s1))
        put(1, 0, t0)
        put(1, 1, t1)
        put(2, 0, jnp.where(low, 0.0, r0))
        put(2, 1, jnp.where(low, r0, r1))

    def shift_cot(h, _):
        put_shifted(g_cot, h, v_cot[h + 1, :, 0:128].astype(F32), v_cot[h + 1, :, 128:256].astype(F32), 1)
        return 0

    bufs = {
        COT: (v_cot, edge.at[0], edge_got.at[0], around.at[0], CH),
        INP: (v_in, edge_in, edge_got_in, around_in, CIN),
        HID: (v_hid, edge.at[1], edge_got.at[1], around.at[1], CH),
        ACT: (v_act, edge.at[2], edge_got.at[2], around.at[2], CH),
    }

    def halo_pack(x):
        v, e, _, _, chans = bufs[x]
        at = iota((chans, 128), 1)

        def pack(h, held):
            t0 = v[h + 1, :, 0:128].astype(F32)
            t1 = v[h + 1, :, 128:256].astype(F32)
            ends = pltpu.roll(jnp.where(at == 127, t1, t0), 2 * h, 1)
            return jnp.where(((at - 2 * h + 1) & 127) < 2, ends, held)

        e[...] = lax.fori_loop(0, FR, pack, jnp.zeros((chans, 128), F32), unroll=8).astype(BF16)

    def halo_copies(x, far):
        v, e, got, _, _ = bufs[x]

        def one(n, src, dst, dr, dc):
            return remote(src, dst, x_send.at[x, n], x_recv.at[x, n], (row_at(dr), col_at(dc)))

        if far:
            return [
                one(2, got.at[0], got.at[2], 1, 0),
                one(3, got.at[1], got.at[3], 1, 0),
                one(4, got.at[0], got.at[4], -1, 0),
                one(5, got.at[1], got.at[5], -1, 0),
            ]
        return [
            one(0, e, got.at[0], 0, 1),
            one(1, e, got.at[1], 0, -1),
            one(6, v.at[FR], v.at[0], 1, 0),
            one(7, v.at[1], v.at[FR + 1], -1, 0),
        ]

    def halo_start(x):
        halo_pack(x)
        for copy in halo_copies(x, False):
            copy.start()

    def set_ring(x, corners):
        _, _, got, ring, chans = bufs[x]
        at = iota((chans, 128), 1)
        top = (r > 0).astype(F32)
        bottom = (r < NR - 1).astype(F32)
        west = (c > 0).astype(F32)
        east = (c < NC - 1).astype(F32)

        def side(mid, up, down, by, by_corner, first, there):
            cells = pltpu.roll(got[mid].astype(F32), by, 1)
            if corners:
                b = pltpu.roll(got[up].astype(F32), by_corner, 1) * top
                d = pltpu.roll(got[down].astype(F32), by_corner, 1) * bottom
                last = (first + 2 * FR + 2) % 128
                cells = jnp.where(at == first, b, jnp.where(at == last, d, cells))
            return cells * there

        both = jnp.where(lax.rem(at, 2) == 0, side(0, 2, 4, 3, 67, 0, west), side(1, 3, 5, 1, 65, 127, east))
        ring[0] = both.astype(BF16)
        ring[1] = pltpu.roll(both, 126, 1).astype(BF16)
        ring[2] = pltpu.roll(both, 124, 1).astype(BF16)

    def halo_near(x):
        v, chans = bufs[x][0], bufs[x][4]
        near = halo_copies(x, False)
        for copy in near[:2]:
            copy.wait()
        for copy in halo_copies(x, True):
            copy.start()
        for copy in near[2:]:
            copy.wait()

        @pl.when(r == 0)
        def _():
            v[0] = jnp.zeros((chans, 256), BF16)

        @pl.when(r == NR - 1)
        def _():
            v[FR + 1] = jnp.zeros((chans, 256), BF16)

    def halo_corners(x):
        for copy in halo_copies(x, True):
            copy.wait()
        set_ring(x, True)

    def combine(prod, n, ends):
        at = iota((n, 128), 1)
        a0, a1 = prod[0:n, 0:128], prod[0:n, 128:256]
        b0, b1 = prod[n : 2 * n, 0:128], prod[n : 2 * n, 128:256]
        d0, d1 = prod[2 * n : 3 * n, 0:128], prod[2 * n : 3 * n, 128:256]
        r0, r1 = pltpu.roll(a0, 1, 1), pltpu.roll(a1, 1, 1)
        s0, s1 = pltpu.roll(d0, 127, 1), pltpu.roll(d1, 127, 1)
        t0 = b0 + jnp.where(at == 0, ends, r0) + jnp.where(at == 127, s1, s0)
        t1 = b1 + jnp.where(at == 0, r0, r1) + jnp.where(at == 127, ends, s1)
        return t0, t1

    def set_fix(x, left, right):
        ring, chans = bufs[x][3], bufs[x][4]
        cells = ring[...].reshape(3 * chans, 128)
        fix[...] = jnp.where(lax.rem(lane, 2) == 0, dot(left, cells), dot(right, cells))

    def fix_of(h):
        return pltpu.roll(fix[...], lax.rem(128 - 2 * h, 128), 1)

    def set_pair_fix(x, weights):
        set_fix(x, weights[0, 0][:, 0 : 3 * CH], weights[2, 0][:, 0 : 3 * CH])

    def conv_pair(weights, v, p):
        prod = dot(weights[...].reshape(6 * CH, 256), v[pl.ds(2 * p, 4)].reshape(256, 256))
        ends = jnp.concatenate([fix_of(2 * p), fix_of(2 * p + 1)], axis=0)
        return combine(prod, 2 * CH, ends)

    halo_pack(COT)

    pl.semaphore_wait(barrier, len(met))

    cs[c] = jnp.full((8, 128), col_start[0], jnp.int32)

    def cs_copy(d):
        return remote(cs.at[c], cs.at[c], cs_send.at[d], cs_recv.at[c], (r, col_at(d)))

    def cs_arrival(d):
        other = col_at(d)
        return remote(cs.at[other], cs.at[other], cs_send.at[d], cs_recv.at[other], (r, other))

    for d in range(1, NC):
        cs_copy(d).start()
    for copy in halo_copies(COT, False):
        copy.start()
    lax.fori_loop(0, FR, shift_cot, 0, unroll=4)
    for d in range(1, NC):
        cs_copy(d).wait_send()
        cs_arrival(d).wait_recv()

    def ag_copy(n):
        to = peer(n)
        return remote(slab.at[to], gath.at[HB + c], ag_send.at[n], ag_recv.at[HB + c], (r, to))

    whole = coarse[...].reshape(256, 256)

    def cut(to):
        pick = one_hot(iota((256, 128), 0) == iota((256, 128), 1) + cs[to][0:1, :])
        return dot(whole, pick).astype(BF16).reshape(4, CH, CW)

    for n in range(NC - 1):
        slab[peer(n)] = cut(peer(n))
        ag_copy(n).start()
    gath[HB + c] = cut(c)

    def set_spot(n, _):
        start = cs[n][0:1, :]
        start = jnp.concatenate([start, start], axis=1)
        spots[n] = one_hot(iota((CW, 256), 1) == iota((CW, 256), 0) + start)
        return 0

    lax.fori_loop(0, NC, set_spot, 0)

    halo_near(COT)
    halo_corners(COT)
    set_pair_fix(COT, wb2)

    def hidden_grad(p, _):
        t0, t1 = conv_pair(wb2, v_cot, p)
        hgrad[pl.ds(2 * p, 2), :, 0:128] = t0.reshape(2, CH, 128)
        hgrad[pl.ds(2 * p, 2), :, 128:256] = t1.reshape(2, CH, 128)
        return 0

    lax.fori_loop(0, FR // 2, hidden_grad, 0, unroll=4)

    def ag_arrival(slot):
        return remote(slab.at[0], gath.at[slot], ag_send.at[0], ag_recv.at[slot], (r, col_at(1)))

    def pass_on(n):
        src, dst, dr = ((NC, 0, 1), (NC + 1, 1, 1), (HB, NC + HB, -1), (HB + 1, NC + HB + 1, -1))[n]
        return remote(gath.at[src], gath.at[dst], ag_send.at[NC + n], ag_recv.at[dst], (row_at(dr), c))

    for n, at in enumerate((NC - 2, NC - 1, 0, 1)):
        @pl.when(c != at)
        def _():
            ag_arrival(HB + at).wait_recv()

        pass_on(n).start()
    for at in range(2, NC - 2):
        @pl.when(c != at)
        def _():
            ag_arrival(HB + at).wait_recv()

    for n in range(NC - 1):
        ag_copy(n).wait_send()
    for n in range(4):
        pass_on(n).wait()

    first_block = r * NC - HB
    for k in range(K):
        piece = gath[jnp.clip(block_ids[0, k] - first_block, 0, NB - 1)]
        for g in range(4):
            pieces[g, 64 * k : 64 * k + 64, :] = piece[:, 16 * g : 16 * g + 16, :].reshape(64, CW)
    for g in range(4):
        sec[:, 16 * g : 16 * g + 16, :] = dot(lmat[...], pieces[g]).astype(BF16).reshape(FR, 16, CW)

    def regrid(q, _):
        flat = sec[pl.ds(4 * q, 4)].reshape(256, CW)
        v_in[pl.ds(1 + 4 * q, 4), FS:CIN, :] = dot(flat, cols[...]).astype(BF16).reshape(4, CH, 256)
        return 0

    lax.fori_loop(0, FR // 4, regrid, 0, unroll=4)

    halo_start(INP)

    def first_row(h, _):
        prod = dot(wf1[:, 0 : 3 * CIN], v_in[pl.ds(h, 3)].reshape(3 * CIN, 256))
        t0, t1 = combine(prod, CH, 0.0)
        pre[h, :, 0:128] = t0
        pre[h, :, 128:256] = t1
        return 0

    lax.fori_loop(1, FR - 1, first_row, 0, unroll=4)

    halo_near(INP)
    set_ring(INP, False)
    first_row(0, 0)
    first_row(FR - 1, 0)

    def set_first_fix():
        set_fix(INP, wf1[0:CH, 0 : 3 * CIN], wf1[2 * CH : 3 * CH, 0 : 3 * CIN])

    set_first_fix()

    def activate(h, _):
        ends = fix_of(h)
        t0 = pre[h, :, 0:128] + jnp.where(lane == 0, ends, 0.0)
        t1 = pre[h, :, 128:256] + jnp.where(lane == 127, ends, 0.0)
        back = []
        for half, t in ((0, t0), (1, t1)):
            at = slice(128 * half, 128 * half + 128)
            s = 1.0 / (1.0 + jnp.exp(-t))
            v_hid[h + 1, :, at] = (t * s).astype(BF16)
            grad = hgrad[h, :, at] * (s * (1.0 + t * (1.0 - s)))
            v_act[h + 1, :, at] = grad.astype(BF16)
            back.append(grad)
        put_shifted(g_act, h, back[0], back[1], 1)
        return 0

    lax.fori_loop(1, FR - 1, activate, 0, unroll=4)
    halo_corners(INP)
    set_first_fix()
    activate(0, 0)
    activate(FR - 1, 0)

    halo_start(ACT)
    halo_start(HID)

    edges = (one_hot(lax.rem(lane, 2) == 0), one_hot(lax.rem(lane, 2) == 1))

    def edge_terms(x, of):
        ring, chans = bufs[x][3], bufs[x][4]
        mine = bufs[of][1][...]
        both = jnp.concatenate([mine * edges[0], mine * edges[1]], axis=0)
        return dot_nt(both, ring[...].reshape(3 * chans, 128))

    acc1[...] = jnp.zeros(acc1.shape, F32)

    def first_grad(h, _):
        acc1[:, 0 : 3 * CIN] += dot_nt(g_act[h].reshape(3 * CH, 256), v_in[pl.ds(h, 3)].reshape(3 * CIN, 256))
        return 0

    lax.fori_loop(0, FR, first_grad, 0, unroll=4)

    extra = edge_terms(INP, ACT)
    acc1[0:CH, 0 : 3 * CIN] += extra[0:CH]
    acc1[2 * CH :, 0 : 3 * CIN] += extra[CH:]

    def w1_copy(which, n):
        to = peer(n)
        return remote(gbuf.at[which, to], gpart.at[which, c], w1_send.at[which, n], w1_recv.at[which, c], (r, to))

    def sum_row(which, acc):
        for half in range(2):
            rows = acc[0 : 3 * CH, 128 * half : 128 * half + 128]
            gbuf[which, 8 * half : 8 * half + 8] = rows.reshape(8, 24, 128)
        for n in range(NC - 1):
            w1_copy(which, n).start()
        gpart[which, c] = gbuf[which, c]

    sum_row(0, acc1)

    halo_near(ACT)
    halo_near(HID)
    halo_corners(HID)
    acc2[...] = jnp.zeros(acc2.shape, F32)

    def second_grad(p, _):
        acc2[...] += dot_nt(g_cot[pl.ds(2 * p, 2)].reshape(6 * CH, 256), v_hid[pl.ds(2 * p, 4)].reshape(256, 256))
        return 0

    lax.fori_loop(0, FR // 2, second_grad, 0, unroll=4)
    extra = edge_terms(HID, COT)
    acc2[0 : 3 * CH, :] += pltpu.roll(acc2[3 * CH :, :], 192, 1)
    acc2[0:CH, 0 : 3 * CH] += extra[0:CH]
    acc2[2 * CH : 3 * CH, 0 : 3 * CH] += extra[CH:]
    sum_row(1, acc2)

    def w2_copy(which, d):
        return remote(
            grow.at[which, r], grow.at[which, r], w2_send.at[which, d], w2_recv.at[which, r], (row_at(d), c)
        )

    def w2_arrival(which, d):
        there = grow.at[which, row_at(d)]
        return remote(there, there, w2_send.at[which, d], w2_recv.at[which, row_at(d)], (row_at(d), c))

    def w3_copy(which, n):
        here = grads_out.at[which, c]
        return remote(here, here, w3_send.at[which, n], w3_recv.at[which, c], (r, peer(n)))

    def w3_arrival(which, n):
        there = grads_out.at[which, source(n)]
        return remote(there, there, w3_send.at[which, n], w3_recv.at[which, source(n)], (r, source(n)))

    def sum_col(which):
        for n in range(NC - 1):
            w1_copy(which, n).wait_send()
            there = gpart.at[which, source(n)]
            remote(there, there, w1_send.at[which, n], w1_recv.at[which, source(n)], (r, source(n))).wait_recv()
        total = gpart[which, 0]
        for n in range(1, NC):
            total = total + gpart[which, n]
        grow[which, r] = total
        for d in range(1, NR):
            w2_copy(which, d).start()

    def spread_sum(which):
        for d in range(1, NR):
            w2_copy(which, d).wait_send()
            w2_arrival(which, d).wait_recv()
        total = grow[which, 0]
        for n in range(1, NR):
            total = total + grow[which, n]
        grads_out[which, c] = total
        for n in range(NC - 1):
            w3_copy(which, n).start()

    set_ring(ACT, False)
    set_pair_fix(ACT, wb1)

    def cond_grad(p, _):
        t0, t1 = conv_pair(wb1, v_act, p)
        fine[pl.ds(2 * p, 2), :, 0:128] = t0.astype(BF16).reshape(2, CH, 128)
        fine[pl.ds(2 * p, 2), :, 128:256] = t1.astype(BF16).reshape(2, CH, 128)
        return 0

    lax.fori_loop(1, FR // 2 - 1, cond_grad, 0, unroll=4)
    halo_corners(ACT)
    set_pair_fix(ACT, wb1)
    cond_grad(0, 0)
    cond_grad(FR // 2 - 1, 0)

    def section_grad(q, _):
        flat = fine[pl.ds(8 * q, 8)].reshape(512, 256)
        sec[pl.ds(8 * q, 8)] = dot_nt(flat, cols[...]).astype(BF16).reshape(8, CH, CW)
        return 0

    lax.fori_loop(0, FR // 8, section_grad, 0)
    eye = one_hot(iota((256, 256), 0) == iota((256, 256), 1))
    lmat_t = dot_nt(eye, lmat[...]).astype(BF16)
    for g in range(4):
        part = dot(lmat_t, sec[:, 16 * g : 16 * g + 16, :].reshape(512, CW))
        pgrad[:, :, 16 * g : 16 * g + 16, :] = part.reshape(K, 4, 16, CW)

    def contribution(b):
        total = None
        for k in range(K):
            hit = (block_ids[0, k] - first_block == b).astype(F32)
            term = pgrad[k] * hit
            total = term if total is None else total + term
        return total

    def rh_copy(n):
        b, dr = ((0, -1), (1, -1), (NB - 2, 1), (NB - 1, 1))[n]
        return remote(sbuf.at[b], rhalo.at[n], rh_send.at[n], rh_recv.at[n], (row_at(dr), c))

    for n, b in enumerate((0, 1, NB - 2, NB - 1)):
        sbuf[b] = contribution(b).astype(BF16)
        rh_copy(n).start()

    def rs_copy(n):
        to = peer(n)
        return remote(sbuf.at[HB + to], rbuf.at[c], rs_send.at[n], rs_recv.at[c], (r, to))

    def is_inner(to):
        return (to >= HB) & (to < NC - HB)

    def send_inner(n):
        to = peer(n)

        @pl.when(is_inner(to))
        def _():
            sbuf[HB + to] = contribution(HB + to).astype(BF16)
            rs_copy(n).start()

    def send_outer(n):
        @pl.when(jnp.logical_not(is_inner(peer(n))))
        def _():
            rs_copy(n).start()

    for n in range(8):
        send_inner(n)
    for n, b in enumerate((NC, NC + 1, HB, HB + 1)):
        rh_copy(n).wait_recv()
        sbuf[b] = (contribution(b) + rhalo[n].astype(F32)).astype(BF16)
    for n in range(8, NC - 1):
        send_inner(n)
        send_outer(n)
        send_outer(n - 8)
    send_outer(7)

    @pl.when(is_inner(c))
    def _():
        sbuf[HB + c] = contribution(HB + c).astype(BF16)

    rbuf[c] = sbuf[HB + c]

    sum_col(0)
    sum_col(1)
    set_pair_fix(HID, wf2)

    def second_level(p, _):
        t0, t1 = conv_pair(wf2, v_hid, p)
        fine[pl.ds(2 * p, 2), :, 0:128] = t0.astype(BF16).reshape(2, CH, 128)
        fine[pl.ds(2 * p, 2), :, 128:256] = t1.astype(BF16).reshape(2, CH, 128)
        return 0

    lax.fori_loop(0, FR // 4, second_level, 0, unroll=4)
    spread_sum(0)
    spread_sum(1)
    lax.fori_loop(FR // 4, FR // 2, second_level, 0, unroll=4)
    out = pltpu.make_async_copy(fine, fine_hbm, out_sem)
    out.start()

    for n in range(NC - 1):
        rs_copy(n).wait_send()
        there = rbuf.at[source(n)]
        remote(there, there, rs_send.at[n], rs_recv.at[source(n)], (r, source(n))).wait_recv()

    def add(q, _):
        flat = [rbuf[4 * q + n].reshape(256, CW) for n in range(4)]
        spot = spots[pl.ds(4 * q, 4)].reshape(4 * CW, 256)
        coarse_out[...] += dot(jnp.concatenate(flat, axis=1), spot).reshape(4, CH, 256)
        return 0

    coarse_out[...] = jnp.zeros((4, CH, 256), F32)
    lax.fori_loop(0, NC // 4, add, 0)

    for n in range(4):
        rh_copy(n).wait_send()
    for which in range(2):
        for n in range(NC - 1):
            w3_copy(which, n).wait_send()
            w3_arrival(which, n).wait_recv()
    out.wait()


def results(
    fine, grads, block, fine_out, first_out, second_out, coarse_out, rows, turned, sums, held, first, second, sem
):
    fetched = pltpu.make_async_copy(block, held, sem.at[0])
    moved = pltpu.make_async_copy(held, coarse_out, sem.at[8])
    arrivals = [
        pltpu.make_async_copy(fine.at[pl.ds(16 * n, 16)], rows.at[pl.ds(16 * n, 16)], sem.at[1 + n]) for n in range(2)
    ]
    summed = pltpu.make_async_copy(grads, sums, sem.at[3])
    leaving = [
        pltpu.make_async_copy(
            turned.at[:, pl.ds(16 * n, 16), :], fine_out.at[:, pl.ds(16 * n, 16), :], sem.at[4 + n]
        )
        for n in range(2)
    ]
    for copy in arrivals:
        copy.start()
    summed.start()
    fetched.start()
    perm = permutation()
    for n in range(2):
        arrivals[n].wait()
        for c0 in range(0, CH, 16):
            flat = rows[16 * n : 16 * n + 16, c0 : c0 + 16, :].reshape(256, 256)
            turned[c0 : c0 + 16, 16 * n : 16 * n + 16, :] = dot(perm, flat).astype(BF16).reshape(16, 16, 256)
        leaving[n].start()
    fetched.wait()
    moved.start()
    summed.wait()
    both = [
        jnp.concatenate([sums[w, 0:8].reshape(3 * CH, 128), sums[w, 8:16].reshape(3 * CH, 128)], axis=1)
        for w in range(2)
    ]
    for a in range(3):
        for e in range(3):
            first[a, e] = both[0][e * CH : (e + 1) * CH, a * CIN : (a + 1) * CIN]
            second[a, e] = both[1][e * CH : (e + 1) * CH, a * CH : (a + 1) * CH]
    last = [
        pltpu.make_async_copy(first, first_out, sem.at[6]),
        pltpu.make_async_copy(second, second_out, sem.at[7]),
    ]
    for copy in last:
        copy.start()
    for copy in leaving + last + [moved]:
        copy.wait()


def local(
    coarse,
    noisy,
    cotangent,
    interp_rows,
    interp_cols,
    first_weight,
    second_weight,
    block_ids,
    weight_ids,
    col_start,
):
    smem = pl.BlockSpec(memory_space=pltpu.SMEM)
    vmem = pl.BlockSpec(memory_space=pltpu.VMEM)
    dma = pltpu.SemaphoreType.DMA
    fine, grads, block = pl.pallas_call(
        kernel,
        out_shape=(
            jax.ShapeDtypeStruct((FR, CH, 256), BF16),
            jax.ShapeDtypeStruct((2, NC, 24, 128), F32),
            jax.ShapeDtypeStruct((4, CH, 256), F32),
        ),
        in_specs=[smem] * 3 + [pl.BlockSpec(memory_space=pl.ANY)] * 7,
        out_specs=(pl.BlockSpec(memory_space=pl.ANY), vmem, vmem),
        scratch_shapes=[
            pltpu.VMEM((4, CH, 256), BF16),
            pltpu.VMEM((FS, FR, 256), BF16),
            pltpu.VMEM((CH, FR, 256), BF16),
            pltpu.VMEM((8, 4, FR), BF16),
            pltpu.VMEM((CW, 256), BF16),
            pltpu.VMEM((3, 3, CH, CIN), BF16),
            pltpu.VMEM((3, 3, CH, CH), BF16),
            pltpu.VMEM((FR + 2, CH, 256), BF16),
            pltpu.VMEM((FR + 2, CIN, 256), BF16),
            pltpu.VMEM((FR + 2, CH, 256), BF16),
            pltpu.VMEM((FR + 2, CH, 256), BF16),
            pltpu.VMEM((FR, 3, CH, 256), BF16),
            pltpu.VMEM((FR, 3, CH, 256), BF16),
            pltpu.VMEM((FR, CH, 256), F32),
            pltpu.VMEM((FR, CH, 256), F32),
            pltpu.VMEM((FR, CH, 256), BF16),
            pltpu.VMEM((3 * CH, 256), BF16),
            pltpu.VMEM((3, 2, CH, 256), BF16),
            pltpu.VMEM((3, 2, CH, 256), BF16),
            pltpu.VMEM((3, 2, CH, 256), BF16),
            pltpu.VMEM((3, CH, 128), BF16),
            pltpu.VMEM((CIN, 128), BF16),
            pltpu.VMEM((3, 6, CH, 128), BF16),
            pltpu.VMEM((6, CIN, 128), BF16),
            pltpu.VMEM((3, 3, CH, 128), BF16),
            pltpu.VMEM((3, CIN, 128), BF16),
            pltpu.VMEM((CH, 128), F32),
            pltpu.VMEM((NC, 8, 128), jnp.int32),
            pltpu.VMEM((NC, 4, CH, CW), BF16),
            pltpu.VMEM((NB, 4, CH, CW), BF16),
            pltpu.VMEM((4, 256, CW), BF16),
            pltpu.VMEM((512, 256), BF16),
            pltpu.VMEM((FR, CH, CW), BF16),
            pltpu.VMEM((K, 4, CH, CW), F32),
            pltpu.VMEM((NB, 4, CH, CW), BF16),
            pltpu.VMEM((NC, 4, CH, CW), BF16),
            pltpu.VMEM((4, 4, CH, CW), BF16),
            pltpu.VMEM((NC, CW, 256), BF16),
            pltpu.VMEM((3 * CH, 256), F32),
            pltpu.VMEM((6 * CH, 256), F32),
            pltpu.VMEM((2, NC, 24, 128), F32),
            pltpu.VMEM((2, NC, 24, 128), F32),
            pltpu.VMEM((2, NR, 24, 128), F32),
            dma((4, 8)),
            dma((4, 8)),
            dma((NC,)),
            dma((NC,)),
            dma((NC + 4,)),
            dma((NB,)),
            dma((NC,)),
            dma((NC,)),
            dma((4,)),
            dma((4,)),
            dma((2, NC)),
            dma((2, NC)),
            dma((2, NR)),
            dma((2, NR)),
            dma((2, NC)),
            dma((2, NC)),
            dma,
            dma((7,)),
        ],
        compiler_params=pltpu.CompilerParams(
            collective_id=0, has_side_effects=True, vmem_limit_bytes=56 * 1024 * 1024
        ),
        cost_estimate=pl.CostEstimate(flops=4_000_000_000, bytes_accessed=8_000_000, transcendentals=524_288),
    )(
        block_ids,
        weight_ids,
        col_start,
        coarse,
        noisy,
        cotangent,
        interp_rows.transpose(0, 2, 1),
        interp_cols,
        first_weight,
        second_weight,
    )
    anywhere = pl.BlockSpec(memory_space=pl.ANY)
    return pl.pallas_call(
        results,
        out_shape=(
            jax.ShapeDtypeStruct((CH, FR, 256), BF16),
            jax.ShapeDtypeStruct((3, 3, CH, CIN), F32),
            jax.ShapeDtypeStruct((3, 3, CH, CH), F32),
            jax.ShapeDtypeStruct((4, CH, 256), F32),
        ),
        in_specs=[anywhere] * 3,
        out_specs=(anywhere,) * 4,
        scratch_shapes=[
            pltpu.VMEM((FR, CH, 256), BF16),
            pltpu.VMEM((CH, FR, 256), BF16),
            pltpu.VMEM((2, NC, 24, 128), F32),
            pltpu.VMEM((4, CH, 256), F32),
            pltpu.VMEM((3, 3, CH, CIN), F32),
            pltpu.VMEM((3, 3, CH, CH), F32),
            dma((9,)),
        ],
        compiler_params=pltpu.CompilerParams(vmem_limit_bytes=60 * 1024 * 1024),
        cost_estimate=pl.CostEstimate(flops=270_000_000, bytes_accessed=4_000_000, transcendentals=0),
    )(fine, grads, block)


def solution(mesh):
    in_specs = (
        P(("row", "col"), None, None),
        P(None, "row", "col"),
        P(None, "row", "col"),
        P(),
        P(),
        P(),
        P(),
        P(("row", "col"), None),
        P(("row", "col"), None),
        P("col"),
    )
    out_specs = (P(None, "row", "col"), P(), P(), P(("row", "col"), None, None))
    return jax.shard_map(local, mesh=mesh, in_specs=in_specs, out_specs=out_specs, check_vma=False)
```

time: 91.3 us -> 82.2 us (0.900)
  Pallas kernels: 84.9 us -> 80 us
  local copies, waits for them, and re-layouts: 4.62 us -> 0 us
    pallas_call x1, Pallas kernels: 82.3 us -> 77.2 us  [local(): pl.pallas_call(kernel, out_shape=(jax.ShapeDtypeStruct((FR, CH, 256), BF1...]
    unnamed x7 -> x0, local copies, waits for them, and re-layouts: 4.62 us -> none
where the time goes in v3:
time: 82.2 us; the launch traced here: 81.5 us
  Pallas kernels  80 us (97%)
  between operations  1.45 us (2%)
    pallas_call x1, Pallas kernels, local(): pl.pallas_call(kernel, out_shape=(jax.ShapeDtypeStruct((FR, CH, 256), BF1...  77.2 us
    pallas_call x1, Pallas kernels, local(): pl.pallas_call(results, out_shape=(jax.ShapeDtypeStruct((CH, FR, 256), BF...  2.8 us

profile of v3, /device:TPU:1, one launch (start us, length us, event | category | flops | bytes accessed | tf_op | source)
XLA Modules:
  0.0 81.5 jit_solution(1358063259691788394)
XLA Ops:
  1.3 77.2 %shard_map.129 = (bf16[32,64,256]{2,1,0:T(8,128)(2,1)}, f32[2,16,24,128]{3,2,1,0:T(8,128)}, f32[4,64,256]{2,1,0:T(8,128)}) custom-call(s32[1,4]{1,0:T(1,128)} %block_ids.1, s32[1,4]{1,0:T(1,128)} %weight_ids.1, s32[1]{0:T(128)S(6)} %copy.14.col_start, bf16[4,64,256]{2,1,0:T(8,128)(2,1)} %rest_0_.1, bf16[16,32,256]{2,1,0:T(8,128)(2,1)} %rest_1_.1, ...), custom_call_target="tpu_custom_call" | custom-call | flops 4000000000 | bytes 8000000 | tf_op jit(solution)/shard_map/pallas_call | solution.py:755
  78.5 2.8 %shard_map.130 = (bf16[64,32,256]{2,1,0:T(8,128)(2,1)}, f32[3,3,64,80]{3,2,1,0:T(8,128)}, f32[3,3,64,64]{3,2,1,0:T(8,128)}, f32[4,64,256]{2,1,0:T(8,128)}) custom-call(bf16[32,64,256]{2,1,0:T(8,128)(2,1)} %get-tuple-element.7.fine, f32[2,16,24,128]{3,2,1,0:T(8,128)} %get-tuple-element.8.grads, f32[4,64,256]{2,1,0:T(8,128)} %get-tuple-element.9.block), custom_call_target="tpu_custom_call" | custom-call | flops 270000000 | bytes 4000000 | tf_op jit(solution)/shard_map/pallas_call | solution.py:844

commit v4 on v3

--- a/solution.py
+++ b/solution.py
@@ -98,8 +98,12 @@
     around_in,
     fix,
     cs,
+    cs_all,
     slab,
-    gath,
+    wide_a,
+    wide_b,
+    gath_a,
+    gath_b,
     pieces,
     lmat,
     sec,
@@ -117,8 +121,12 @@
     x_recv,
     cs_send,
     cs_recv,
-    ag_send,
-    ag_recv,
+    s1_send,
+    s1_recv,
+    s2_send,
+    s2_recv,
+    po_send,
+    po_recv,
     rs_send,
     rs_recv,
     rh_send,
@@ -346,44 +354,95 @@
 
     cs[c] = jnp.full((8, 128), col_start[0], jnp.int32)
 
-    def cs_copy(d):
-        return remote(cs.at[c], cs.at[c], cs_send.at[d], cs_recv.at[c], (r, col_at(d)))
-
-    def cs_arrival(d):
-        other = col_at(d)
-        return remote(cs.at[other], cs.at[other], cs_send.at[d], cs_recv.at[other], (r, other))
-
-    for d in range(1, NC):
-        cs_copy(d).start()
+    cx, cy = lax.div(c, 4), lax.rem(c, 4)
+
+    def line(axis, d):
+        return lax.rem(cx + d, 4) * 4 + cy if axis == 0 else cx * 4 + lax.rem(cy + d, 4)
+
+    mine = (cx, cy)
+    wide = (wide_a, wide_b)
+    tight = (gath_a, gath_b)
+
+    def s1_copy(axis, d):
+        here = mine[axis]
+        return remote(
+            coarse.at[pl.ds(2 * axis, 2)],
+            wide[axis].at[here],
+            s1_send.at[axis, d],
+            s1_recv.at[axis, here],
+            (r, line(axis, d)),
+        )
+
+    def s1_arrival(axis, d):
+        there = lax.rem(mine[axis] + d, 4)
+        ref = wide[axis].at[there]
+        return remote(ref, ref, s1_send.at[axis, d], s1_recv.at[axis, there], (r, line(axis, d)))
+
+    def cs_copy(axis, d):
+        return remote(
+            cs.at[c], cs.at[c], cs_send.at[axis, d], cs_recv.at[axis, mine[axis]], (r, line(axis, d))
+        )
+
+    def cs_arrival(axis, d):
+        ref = cs.at[line(axis, d)]
+        there = lax.rem(mine[axis] + d, 4)
+        return remote(ref, ref, cs_send.at[axis, d], cs_recv.at[axis, there], (r, line(axis, d)))
+
+    def group_copy(d):
+        group = pl.ds(4 * cx, 4)
+        return remote(cs.at[group], cs_all.at[group], cs_send.at[2, d], cs_recv.at[2, cx], (r, line(0, d)))
+
+    def group_arrival(d):
+        there = lax.rem(cx + d, 4)
+        ref = cs_all.at[pl.ds(4 * there, 4)]
+        return remote(ref, ref, cs_send.at[2, d], cs_recv.at[2, there], (r, line(0, d)))
+
+    for d in (2, 1, 3):
+        for axis in range(2):
+            cs_copy(axis, d).start()
+    for d in (2, 1, 3):
+        for axis in range(2):
+            s1_copy(axis, d).start()
+    for axis in range(2):
+        wide[axis][mine[axis]] = coarse[2 * axis : 2 * axis + 2]
     for copy in halo_copies(COT, False):
         copy.start()
     lax.fori_loop(0, FR, shift_cot, 0, unroll=4)
-    for d in range(1, NC):
-        cs_copy(d).wait_send()
-        cs_arrival(d).wait_recv()
-
-    def ag_copy(n):
-        to = peer(n)
-        return remote(slab.at[to], gath.at[HB + c], ag_send.at[n], ag_recv.at[HB + c], (r, to))
-
-    whole = coarse[...].reshape(256, 256)
-
-    def cut(to):
+    for axis in (1, 0):
+        for d in range(1, 4):
+            cs_copy(axis, d).wait_send()
+            cs_arrival(axis, d).wait_recv()
+    cs_all[pl.ds(4 * cx, 4)] = cs[pl.ds(4 * cx, 4)]
+
+    def s2_copy(axis, d):
+        here = mine[1 - axis]
+        return remote(
+            slab.at[axis, d],
+            tight[axis].at[pl.ds(4 * here, 4)],
+            s2_send.at[axis, d],
+            s2_recv.at[axis, here],
+            (r, line(1 - axis, d)),
+        )
+
+    def s2_arrival(axis, d):
+        there = lax.rem(mine[1 - axis] + d, 4)
+        ref = tight[axis].at[pl.ds(4 * there, 4)]
+        return remote(ref, ref, s2_send.at[axis, d], s2_recv.at[axis, there], (r, line(1 - axis, d)))
+
+    def cut(axis, to):
         pick = one_hot(iota((256, 128), 0) == iota((256, 128), 1) + cs[to][0:1, :])
-        return dot(whole, pick).astype(BF16).reshape(4, CH, CW)
-
-    for n in range(NC - 1):
-        slab[peer(n)] = cut(peer(n))
-        ag_copy(n).start()
-    gath[HB + c] = cut(c)
-
-    def set_spot(n, _):
-        start = cs[n][0:1, :]
-        start = jnp.concatenate([start, start], axis=1)
-        spots[n] = one_hot(iota((CW, 256), 1) == iota((CW, 256), 0) + start)
-        return 0
-
-    lax.fori_loop(0, NC, set_spot, 0)
+        return dot(wide[axis][...].reshape(512, 256), pick).astype(BF16).reshape(4, 2, CH, CW)
+
+    for axis in range(2):
+        for d in range(1, 4):
+            s1_arrival(axis, d).wait_recv()
+        for d in (2, 1, 3):
+            slab[axis, d] = cut(axis, line(1 - axis, d))
+            s2_copy(axis, d).start()
+    for d in (2, 1, 3):
+        group_copy(d).start()
+    for axis in range(2):
+        tight[axis][pl.ds(4 * mine[1 - axis], 4)] = cut(axis, c)
 
     halo_near(COT)
     halo_corners(COT)
@@ -397,34 +456,57 @@
 
     lax.fori_loop(0, FR // 2, hidden_grad, 0, unroll=4)
 
-    def ag_arrival(slot):
-        return remote(slab.at[0], gath.at[slot], ag_send.at[0], ag_recv.at[slot], (r, col_at(1)))
+    for d in range(1, 4):
+        group_copy(d).wait_send()
+        group_arrival(d).wait_recv()
+
+    def set_spot(n, _):
+        start = cs_all[n][0:1, :]
+        start = jnp.concatenate([start, start], axis=1)
+        spots[n] = one_hot(iota((CW, 256), 1) == iota((CW, 256), 0) + start)
+        return 0
+
+    lax.fori_loop(0, NC, set_spot, 0)
+
+    for axis in range(2):
+        for d in range(1, 4):
+            s1_copy(axis, d).wait_send()
+            s2_copy(axis, d).wait_send()
+            s2_arrival(axis, d).wait_recv()
 
     def pass_on(n):
-        src, dst, dr = ((NC, 0, 1), (NC + 1, 1, 1), (HB, NC + HB, -1), (HB + 1, NC + HB + 1, -1))[n]
-        return remote(gath.at[src], gath.at[dst], ag_send.at[NC + n], ag_recv.at[dst], (row_at(dr), c))
-
-    for n, at in enumerate((NC - 2, NC - 1, 0, 1)):
-        @pl.when(c != at)
-        def _():
-            ag_arrival(HB + at).wait_recv()
-
+        half, src, dst, count, dr = (
+            (0, 11, NC, 1, 1),
+            (0, 15, NC + 1, 1, 1),
+            (0, 0, NC + 2, 1, -1),
+            (0, 4, NC + 3, 1, -1),
+            (1, 14, NC, 2, 1),
+            (1, 0, NC + 2, 2, -1),
+        )[n]
+        return remote(
+            tight[half].at[pl.ds(src, count)],
+            tight[half].at[pl.ds(dst, count)],
+            po_send.at[n],
+            po_recv.at[n],
+            (row_at(dr), c),
+        )
+
+    for n in range(6):
         pass_on(n).start()
-    for at in range(2, NC - 2):
-        @pl.when(c != at)
-        def _():
-            ag_arrival(HB + at).wait_recv()
-
-    for n in range(NC - 1):
-        ag_copy(n).wait_send()
-    for n in range(4):
+    for n in range(6):
         pass_on(n).wait()
 
     first_block = r * NC - HB
     for k in range(K):
-        piece = gath[jnp.clip(block_ids[0, k] - first_block, 0, NB - 1)]
-        for g in range(4):
-            pieces[g, 64 * k : 64 * k + 64, :] = piece[:, 16 * g : 16 * g + 16, :].reshape(64, CW)
+        near = jnp.clip(block_ids[0, k] - first_block, 0, NB - 1)
+        own = jnp.clip(near - HB, 0, NC - 1)
+        outer = jnp.where(near < HB, NC + near, near)
+        inside = (near >= HB) & (near < NC + HB)
+        for half, at in ((0, lax.rem(own, 4) * 4 + lax.div(own, 4)), (1, own)):
+            piece = tight[half][jnp.where(inside, at, outer)]
+            for g in range(4):
+                row = 64 * k + 32 * half
+                pieces[g, row : row + 32, :] = piece[:, 16 * g : 16 * g + 16, :].reshape(32, CW)
     for g in range(4):
         sec[:, 16 * g : 16 * g + 16, :] = dot(lmat[...], pieces[g]).astype(BF16).reshape(FR, 16, CW)
 
@@ -490,85 +572,87 @@
 
     acc1[...] = jnp.zeros(acc1.shape, F32)
 
-    def first_grad(h, _):
-        acc1[:, 0 : 3 * CIN] += dot_nt(g_act[h].reshape(3 * CH, 256), v_in[pl.ds(h, 3)].reshape(3 * CIN, 256))
-        return 0
-
-    lax.fori_loop(0, FR, first_grad, 0, unroll=4)
+    def first_grad(q, _):
+        left = [g_act[4 * q + i].reshape(3 * CH, 256) for i in range(4)]
+        right = [v_in[pl.ds(4 * q + i, 3)].reshape(3 * CIN, 256) for i in range(4)]
+        acc1[:, 0 : 3 * CIN] += dot_nt(jnp.concatenate(left, axis=1), jnp.concatenate(right, axis=1))
+        return 0
+
+    lax.fori_loop(0, FR // 4, first_grad, 0, unroll=2)
 
     extra = edge_terms(INP, ACT)
     acc1[0:CH, 0 : 3 * CIN] += extra[0:CH]
     acc1[2 * CH :, 0 : 3 * CIN] += extra[CH:]
 
-    def w1_copy(which, n):
+    def w1_copy(n):
         to = peer(n)
-        return remote(gbuf.at[which, to], gpart.at[which, c], w1_send.at[which, n], w1_recv.at[which, c], (r, to))
-
-    def sum_row(which, acc):
+        return remote(gbuf.at[to], gpart.at[c], w1_send.at[n], w1_recv.at[c], (r, to))
+
+    def keep(which, acc):
         for half in range(2):
             rows = acc[0 : 3 * CH, 128 * half : 128 * half + 128]
-            gbuf[which, 8 * half : 8 * half + 8] = rows.reshape(8, 24, 128)
-        for n in range(NC - 1):
-            w1_copy(which, n).start()
-        gpart[which, c] = gbuf[which, c]
-
-    sum_row(0, acc1)
+            gbuf[8 * half : 8 * half + 8, which] = rows.reshape(8, 24, 128)
+
+    keep(0, acc1)
 
     halo_near(ACT)
     halo_near(HID)
     halo_corners(HID)
     acc2[...] = jnp.zeros(acc2.shape, F32)
 
-    def second_grad(p, _):
-        acc2[...] += dot_nt(g_cot[pl.ds(2 * p, 2)].reshape(6 * CH, 256), v_hid[pl.ds(2 * p, 4)].reshape(256, 256))
-        return 0
-
-    lax.fori_loop(0, FR // 2, second_grad, 0, unroll=4)
+    def second_grad(q, _):
+        left = [g_cot[pl.ds(4 * q + i, 2)].reshape(6 * CH, 256) for i in (0, 2)]
+        right = [v_hid[pl.ds(4 * q + i, 4)].reshape(256, 256) for i in (0, 2)]
+        acc2[...] += dot_nt(jnp.concatenate(left, axis=1), jnp.concatenate(right, axis=1))
+        return 0
+
+    lax.fori_loop(0, FR // 4, second_grad, 0, unroll=2)
     extra = edge_terms(HID, COT)
     acc2[0 : 3 * CH, :] += pltpu.roll(acc2[3 * CH :, :], 192, 1)
     acc2[0:CH, 0 : 3 * CH] += extra[0:CH]
     acc2[2 * CH : 3 * CH, 0 : 3 * CH] += extra[CH:]
-    sum_row(1, acc2)
-
-    def w2_copy(which, d):
-        return remote(
-            grow.at[which, r], grow.at[which, r], w2_send.at[which, d], w2_recv.at[which, r], (row_at(d), c)
-        )
-
-    def w2_arrival(which, d):
-        there = grow.at[which, row_at(d)]
-        return remote(there, there, w2_send.at[which, d], w2_recv.at[which, row_at(d)], (row_at(d), c))
-
-    def w3_copy(which, n):
-        here = grads_out.at[which, c]
-        return remote(here, here, w3_send.at[which, n], w3_recv.at[which, c], (r, peer(n)))
-
-    def w3_arrival(which, n):
-        there = grads_out.at[which, source(n)]
-        return remote(there, there, w3_send.at[which, n], w3_recv.at[which, source(n)], (r, source(n)))
-
-    def sum_col(which):
+    keep(1, acc2)
+    for n in range(NC - 1):
+        w1_copy(n).start()
+    gpart[c] = gbuf[c]
+
+    def w2_copy(d):
+        return remote(grow.at[r], grow.at[r], w2_send.at[d], w2_recv.at[r], (row_at(d), c))
+
+    def w2_arrival(d):
+        there = grow.at[row_at(d)]
+        return remote(there, there, w2_send.at[d], w2_recv.at[row_at(d)], (row_at(d), c))
+
+    def w3_copy(n):
+        here = grads_out.at[c]
+        return remote(here, here, w3_send.at[n], w3_recv.at[c], (r, peer(n)))
+
+    def w3_arrival(n):
+        there = grads_out.at[source(n)]
+        return remote(there, there, w3_send.at[n], w3_recv.at[source(n)], (r, source(n)))
+
+    def sum_col():
         for n in range(NC - 1):
-            w1_copy(which, n).wait_send()
-            there = gpart.at[which, source(n)]
-            remote(there, there, w1_send.at[which, n], w1_recv.at[which, source(n)], (r, source(n))).wait_recv()
-        total = gpart[which, 0]
+            w1_copy(n).wait_send()
+            there = gpart.at[source(n)]
+            remote(there, there, w1_send.at[n], w1_recv.at[source(n)], (r, source(n))).wait_recv()
+        total = gpart[0]
         for n in range(1, NC):
-            total = total + gpart[which, n]
-        grow[which, r] = total
+            total = total + gpart[n]
+        grow[r] = total
         for d in range(1, NR):
-            w2_copy(which, d).start()
-
-    def spread_sum(which):
+            w2_copy(d).start()
+
+    def spread_sum():
         for d in range(1, NR):
-            w2_copy(which, d).wait_send()
-            w2_arrival(which, d).wait_recv()
-        total = grow[which, 0]
+            w2_copy(d).wait_send()
+            w2_arrival(d).wait_recv()
+        total = grow[0]
         for n in range(1, NR):
-            total = total + grow[which, n]
-        grads_out[which, c] = total
+            total = total + grow[n]
+        grads_out[c] = total
         for n in range(NC - 1):
-            w3_copy(which, n).start()
+            w3_copy(n).start()
 
     set_ring(ACT, False)
     set_pair_fix(ACT, wb1)
@@ -650,8 +734,7 @@
 
     rbuf[c] = sbuf[HB + c]
 
-    sum_col(0)
-    sum_col(1)
+    sum_col()
     set_pair_fix(HID, wf2)
 
     def second_level(p, _):
@@ -661,32 +744,27 @@
         return 0
 
     lax.fori_loop(0, FR // 4, second_level, 0, unroll=4)
-    spread_sum(0)
-    spread_sum(1)
+    spread_sum()
     lax.fori_loop(FR // 4, FR // 2, second_level, 0, unroll=4)
     out = pltpu.make_async_copy(fine, fine_hbm, out_sem)
     out.start()
 
-    for n in range(NC - 1):
-        rs_copy(n).wait_send()
-        there = rbuf.at[source(n)]
-        remote(there, there, rs_send.at[n], rs_recv.at[source(n)], (r, source(n))).wait_recv()
-
-    def add(q, _):
-        flat = [rbuf[4 * q + n].reshape(256, CW) for n in range(4)]
-        spot = spots[pl.ds(4 * q, 4)].reshape(4 * CW, 256)
-        coarse_out[...] += dot(jnp.concatenate(flat, axis=1), spot).reshape(4, CH, 256)
-        return 0
-
-    coarse_out[...] = jnp.zeros((4, CH, 256), F32)
-    lax.fori_loop(0, NC // 4, add, 0)
+    for q in range(4):
+        senders = [source(n) if n < NC - 1 else c for n in range(4 * q, 4 * q + 4)]
+        for n in range(4 * q, min(4 * q + 4, NC - 1)):
+            rs_copy(n).wait_send()
+            there = rbuf.at[source(n)]
+            remote(there, there, rs_send.at[n], rs_recv.at[source(n)], (r, source(n))).wait_recv()
+        flat = jnp.concatenate([rbuf[n].reshape(256, CW) for n in senders], axis=1)
+        spot = jnp.concatenate([spots[n] for n in senders], axis=0)
+        part = dot(flat, spot).reshape(4, CH, 256)
+        coarse_out[...] = part if q == 0 else coarse_out[...] + part
 
     for n in range(4):
         rh_copy(n).wait_send()
-    for which in range(2):
-        for n in range(NC - 1):
-            w3_copy(which, n).wait_send()
-            w3_arrival(which, n).wait_recv()
+    for n in range(NC - 1):
+        w3_copy(n).wait_send()
+        w3_arrival(n).wait_recv()
     out.wait()
 
 
@@ -720,7 +798,7 @@
     moved.start()
     summed.wait()
     both = [
-        jnp.concatenate([sums[w, 0:8].reshape(3 * CH, 128), sums[w, 8:16].reshape(3 * CH, 128)], axis=1)
+        jnp.concatenate([sums[0:8, w].reshape(3 * CH, 128), sums[8:16, w].reshape(3 * CH, 128)], axis=1)
         for w in range(2)
     ]
     for a in range(3):
@@ -756,7 +834,7 @@
         kernel,
         out_shape=(
             jax.ShapeDtypeStruct((FR, CH, 256), BF16),
-            jax.ShapeDtypeStruct((2, NC, 24, 128), F32),
+            jax.ShapeDtypeStruct((NC, 2, 24, 128), F32),
             jax.ShapeDtypeStruct((4, CH, 256), F32),
         ),
         in_specs=[smem] * 3 + [pl.BlockSpec(memory_space=pl.ANY)] * 7,
@@ -790,8 +868,12 @@
             pltpu.VMEM((3, CIN, 128), BF16),
             pltpu.VMEM((CH, 128), F32),
             pltpu.VMEM((NC, 8, 128), jnp.int32),
-            pltpu.VMEM((NC, 4, CH, CW), BF16),
-            pltpu.VMEM((NB, 4, CH, CW), BF16),
+            pltpu.VMEM((NC, 8, 128), jnp.int32),
+            pltpu.VMEM((2, 4, 4, 2, CH, CW), BF16),
+            pltpu.VMEM((4, 2, CH, 256), BF16),
+            pltpu.VMEM((4, 2, CH, 256), BF16),
+            pltpu.VMEM((NB, 2, CH, CW), BF16),
+            pltpu.VMEM((NB, 2, CH, CW), BF16),
             pltpu.VMEM((4, 256, CW), BF16),
             pltpu.VMEM((512, 256), BF16),
             pltpu.VMEM((FR, CH, CW), BF16),
@@ -802,25 +884,29 @@
             pltpu.VMEM((NC, CW, 256), BF16),
             pltpu.VMEM((3 * CH, 256), F32),
             pltpu.VMEM((6 * CH, 256), F32),
-            pltpu.VMEM((2, NC, 24, 128), F32),
-            pltpu.VMEM((2, NC, 24, 128), F32),
-            pltpu.VMEM((2, NR, 24, 128), F32),
+            pltpu.VMEM((NC, 2, 24, 128), F32),
+            pltpu.VMEM((NC, 2, 24, 128), F32),
+            pltpu.VMEM((NR, 2, 24, 128), F32),
             dma((4, 8)),
             dma((4, 8)),
-            dma((NC,)),
-            dma((NC,)),
-            dma((NC + 4,)),
-            dma((NB,)),
+            dma((3, 4)),
+            dma((3, 4)),
+            dma((2, 4)),
+            dma((2, 4)),
+            dma((2, 4)),
+            dma((2, 4)),
+            dma((6,)),
+            dma((6,)),
             dma((NC,)),
             dma((NC,)),
             dma((4,)),
             dma((4,)),
-            dma((2, NC)),
-            dma((2, NC)),
-            dma((2, NR)),
-            dma((2, NR)),
-            dma((2, NC)),
-            dma((2, NC)),
+            dma((NC,)),
+            dma((NC,)),
+            dma((NR,)),
+            dma((NR,)),
+            dma((NC,)),
+            dma((NC,)),
             dma,
             dma((7,)),
         ],
@@ -854,7 +940,7 @@
         scratch_shapes=[
             pltpu.VMEM((FR, CH, 256), BF16),
             pltpu.VMEM((CH, FR, 256), BF16),
-            pltpu.VMEM((2, NC, 24, 128), F32),
+            pltpu.VMEM((NC, 2, 24, 128), F32),
             pltpu.VMEM((4, CH, 256), F32),
             pltpu.VMEM((3, 3, CH, CIN), F32),
             pltpu.VMEM((3, 3, CH, CH), F32),

time: 82.2 us -> 78.3 us (0.953)
  Pallas kernels: 80 us -> 76.7 us
    pallas_call x1, Pallas kernels: 77.2 us -> 73.9 us  [local(): pl.pallas_call(kernel, out_shape=(jax.ShapeDtypeStruct((FR, CH, 256), BF1...]
where the time goes in v4:
time: 78.3 us; the launch traced here: 78.2 us
  Pallas kernels  76.7 us (98%)
  between operations  1.45 us (2%)
    pallas_call x1, Pallas kernels, local(): pl.pallas_call(kernel, out_shape=(jax.ShapeDtypeStruct((FR, CH, 256), BF1...  73.9 us
    pallas_call x1, Pallas kernels, local(): pl.pallas_call(results, out_shape=(jax.ShapeDtypeStruct((CH, FR, 256), BF...  2.8 us

profile of v4, /device:TPU:1, one launch (start us, length us, event | category | flops | bytes accessed | tf_op | source)
XLA Modules:
  0.0 78.2 jit_solution(8537837330979181908)
XLA Ops:
  1.3 73.9 %shard_map.129 = (bf16[32,64,256]{2,1,0:T(8,128)(2,1)}, f32[16,2,24,128]{3,2,1,0:T(8,128)}, f32[4,64,256]{2,1,0:T(8,128)}) custom-call(s32[1,4]{1,0:T(1,128)} %block_ids.1, s32[1,4]{1,0:T(1,128)} %weight_ids.1, s32[1]{0:T(128)S(6)} %copy.14.col_start, bf16[4,64,256]{2,1,0:T(8,128)(2,1)} %rest_0_.1, bf16[16,32,256]{2,1,0:T(8,128)(2,1)} %rest_1_.1, ...), custom_call_target="tpu_custom_call" | custom-call | flops 4000000000 | bytes 8000000 | tf_op jit(solution)/shard_map/pallas_call | solution.py:833
  75.2 2.8 %shard_map.130 = (bf16[64,32,256]{2,1,0:T(8,128)(2,1)}, f32[3,3,64,80]{3,2,1,0:T(8,128)}, f32[3,3,64,64]{3,2,1,0:T(8,128)}, f32[4,64,256]{2,1,0:T(8,128)}) custom-call(bf16[32,64,256]{2,1,0:T(8,128)(2,1)} %get-tuple-element.7.fine, f32[16,2,24,128]{3,2,1,0:T(8,128)} %get-tuple-element.8.grads, f32[4,64,256]{2,1,0:T(8,128)} %get-tuple-element.9.block), custom_call_target="tpu_custom_call" | custom-call | flops 270000000 | bytes 4000000 | tf_op jit(solution)/shard_map/pallas_call | solution.py:930

commit v5 on v4

--- a/solution.py
+++ b/solution.py
@@ -559,8 +559,8 @@
     activate(0, 0)
     activate(FR - 1, 0)
 
+    halo_start(HID)
     halo_start(ACT)
-    halo_start(HID)
 
     edges = (one_hot(lax.rem(lane, 2) == 0), one_hot(lax.rem(lane, 2) == 1))
 
@@ -595,9 +595,7 @@
 
     keep(0, acc1)
 
-    halo_near(ACT)
     halo_near(HID)
-    halo_corners(HID)
     acc2[...] = jnp.zeros(acc2.shape, F32)
 
     def second_grad(q, _):
@@ -607,6 +605,8 @@
         return 0
 
     lax.fori_loop(0, FR // 4, second_grad, 0, unroll=2)
+    halo_near(ACT)
+    halo_corners(HID)
     extra = edge_terms(HID, COT)
     acc2[0 : 3 * CH, :] += pltpu.roll(acc2[3 * CH :, :], 192, 1)
     acc2[0:CH, 0 : 3 * CH] += extra[0:CH]
@@ -746,7 +746,11 @@
     lax.fori_loop(0, FR // 4, second_level, 0, unroll=4)
     spread_sum()
     lax.fori_loop(FR // 4, FR // 2, second_level, 0, unroll=4)
-    out = pltpu.make_async_copy(fine, fine_hbm, out_sem)
+    for c0 in range(0, CH, 16):
+        for h0 in range(0, FR, 16):
+            flat = fine[h0 : h0 + 16, c0 : c0 + 16, :].reshape(256, 256)
+            cot[c0 : c0 + 16, h0 : h0 + 16, :] = dot(perm, flat).astype(BF16).reshape(16, 16, 256)
+    out = pltpu.make_async_copy(cot, fine_hbm, out_sem)
     out.start()
 
     for q in range(4):
@@ -768,31 +772,19 @@
     out.wait()
 
 
-def results(
-    fine, grads, block, fine_out, first_out, second_out, coarse_out, rows, turned, sums, held, first, second, sem
-):
+def results(fine, grads, block, fine_out, first_out, second_out, coarse_out, rows, sums, held, first, second, sem):
     fetched = pltpu.make_async_copy(block, held, sem.at[0])
-    moved = pltpu.make_async_copy(held, coarse_out, sem.at[8])
-    arrivals = [
-        pltpu.make_async_copy(fine.at[pl.ds(16 * n, 16)], rows.at[pl.ds(16 * n, 16)], sem.at[1 + n]) for n in range(2)
-    ]
-    summed = pltpu.make_async_copy(grads, sums, sem.at[3])
-    leaving = [
-        pltpu.make_async_copy(
-            turned.at[:, pl.ds(16 * n, 16), :], fine_out.at[:, pl.ds(16 * n, 16), :], sem.at[4 + n]
-        )
-        for n in range(2)
-    ]
+    moved = pltpu.make_async_copy(held, coarse_out, sem.at[1])
+    summed = pltpu.make_async_copy(grads, sums, sem.at[2])
+    parts = [pl.ds(16 * n, 16) for n in range(4)]
+    arrivals = [pltpu.make_async_copy(fine.at[p], rows.at[p], sem.at[5 + n]) for n, p in enumerate(parts)]
+    leaving = [pltpu.make_async_copy(rows.at[p], fine_out.at[p], sem.at[9 + n]) for n, p in enumerate(parts)]
+    summed.start()
     for copy in arrivals:
         copy.start()
-    summed.start()
     fetched.start()
-    perm = permutation()
-    for n in range(2):
+    for n in range(4):
         arrivals[n].wait()
-        for c0 in range(0, CH, 16):
-            flat = rows[16 * n : 16 * n + 16, c0 : c0 + 16, :].reshape(256, 256)
-            turned[c0 : c0 + 16, 16 * n : 16 * n + 16, :] = dot(perm, flat).astype(BF16).reshape(16, 16, 256)
         leaving[n].start()
     fetched.wait()
     moved.start()
@@ -806,8 +798,8 @@
             first[a, e] = both[0][e * CH : (e + 1) * CH, a * CIN : (a + 1) * CIN]
             second[a, e] = both[1][e * CH : (e + 1) * CH, a * CH : (a + 1) * CH]
     last = [
-        pltpu.make_async_copy(first, first_out, sem.at[6]),
-        pltpu.make_async_copy(second, second_out, sem.at[7]),
+        pltpu.make_async_copy(first, first_out, sem.at[3]),
+        pltpu.make_async_copy(second, second_out, sem.at[4]),
     ]
     for copy in last:
         copy.start()
@@ -833,7 +825,7 @@
     fine, grads, block = pl.pallas_call(
         kernel,
         out_shape=(
-            jax.ShapeDtypeStruct((FR, CH, 256), BF16),
+            jax.ShapeDtypeStruct((CH, FR, 256), BF16),
             jax.ShapeDtypeStruct((NC, 2, 24, 128), F32),
             jax.ShapeDtypeStruct((4, CH, 256), F32),
         ),
@@ -938,13 +930,12 @@
         in_specs=[anywhere] * 3,
         out_specs=(anywhere,) * 4,
         scratch_shapes=[
-            pltpu.VMEM((FR, CH, 256), BF16),
             pltpu.VMEM((CH, FR, 256), BF16),
             pltpu.VMEM((NC, 2, 24, 128), F32),
             pltpu.VMEM((4, CH, 256), F32),
             pltpu.VMEM((3, 3, CH, CIN), F32),
             pltpu.VMEM((3, 3, CH, CH), F32),
-            dma((9,)),
+            dma((13,)),
         ],
         compiler_params=pltpu.CompilerParams(vmem_limit_bytes=60 * 1024 * 1024),
         cost_estimate=pl.CostEstimate(flops=270_000_000, bytes_accessed=4_000_000, transcendentals=0),

time: 78.3 us -> 76 us (0.971)
  Pallas kernels: 76.7 us -> 74.3 us
    pallas_call x1, Pallas kernels: 73.9 us -> 71.9 us  [local(): pl.pallas_call(kernel, out_shape=(jax.ShapeDtypeStruct((CH, FR, 256), BF1...]
where the time goes in v5:
time: 76 us; the launch traced here: 75.8 us
  Pallas kernels  74.3 us (98%)
  between operations  1.45 us (2%)
    pallas_call x1, Pallas kernels, local(): pl.pallas_call(kernel, out_shape=(jax.ShapeDtypeStruct((CH, FR, 256), BF1...  71.9 us
    pallas_call x1, Pallas kernels, local(): pl.pallas_call(results, out_shape=(jax.ShapeDtypeStruct((CH, FR, 256), BF...  2.47 us

profile of v5, /device:TPU:1, one launch (start us, length us, event | category | flops | bytes accessed | tf_op | source)
XLA Modules:
  0.0 75.8 jit_solution(2400589557258785108)
XLA Ops:
  1.3 71.9 %shard_map.129 = (bf16[64,32,256]{2,1,0:T(8,128)(2,1)}, f32[16,2,24,128]{3,2,1,0:T(8,128)}, f32[4,64,256]{2,1,0:T(8,128)}) custom-call(s32[1,4]{1,0:T(1,128)} %block_ids.1, s32[1,4]{1,0:T(1,128)} %weight_ids.1, s32[1]{0:T(128)S(6)} %copy.14.col_start, bf16[4,64,256]{2,1,0:T(8,128)(2,1)} %rest_0_.1, bf16[16,32,256]{2,1,0:T(8,128)(2,1)} %rest_1_.1, ...), custom_call_target="tpu_custom_call" | custom-call | flops 4000000000 | bytes 8000000 | tf_op jit(solution)/shard_map/pallas_call | solution.py:825
  73.1 2.5 %shard_map.130 = (bf16[64,32,256]{2,1,0:T(8,128)(2,1)}, f32[3,3,64,80]{3,2,1,0:T(8,128)}, f32[3,3,64,64]{3,2,1,0:T(8,128)}, f32[4,64,256]{2,1,0:T(8,128)}) custom-call(bf16[64,32,256]{2,1,0:T(8,128)(2,1)} %get-tuple-element.7.fine, f32[16,2,24,128]{3,2,1,0:T(8,128)} %get-tuple-element.8.grads, f32[4,64,256]{2,1,0:T(8,128)} %get-tuple-element.9.block), custom_call_target="tpu_custom_call" | custom-call | flops 270000000 | bytes 4000000 | tf_op jit(solution)/shard_map/pallas_call | solution.py:922

commit v6 on v5

--- a/solution.py
+++ b/solution.py
@@ -351,6 +351,8 @@
     halo_pack(COT)
 
     pl.semaphore_wait(barrier, len(met))
+    for copy in halo_copies(COT, False):
+        copy.start()
 
     cs[c] = jnp.full((8, 128), col_start[0], jnp.int32)
 
@@ -405,8 +407,6 @@
             s1_copy(axis, d).start()
     for axis in range(2):
         wide[axis][mine[axis]] = coarse[2 * axis : 2 * axis + 2]
-    for copy in halo_copies(COT, False):
-        copy.start()
     lax.fori_loop(0, FR, shift_cot, 0, unroll=4)
     for axis in (1, 0):
         for d in range(1, 4):
@@ -445,8 +445,6 @@
         tight[axis][pl.ds(4 * mine[1 - axis], 4)] = cut(axis, c)
 
     halo_near(COT)
-    halo_corners(COT)
-    set_pair_fix(COT, wb2)
 
     def hidden_grad(p, _):
         t0, t1 = conv_pair(wb2, v_cot, p)
@@ -454,7 +452,6 @@
         hgrad[pl.ds(2 * p, 2), :, 128:256] = t1.reshape(2, CH, 128)
         return 0
 
-    lax.fori_loop(0, FR // 2, hidden_grad, 0, unroll=4)
 
     for d in range(1, 4):
         group_copy(d).wait_send()
@@ -493,6 +490,9 @@
 
     for n in range(6):
         pass_on(n).start()
+    halo_corners(COT)
+    set_pair_fix(COT, wb2)
+    lax.fori_loop(0, FR // 2, hidden_grad, 0, unroll=4)
     for n in range(6):
         pass_on(n).wait()
 

time: 76 us -> 76.1 us (level)
  no operation moved by 1% of the time
where the time goes in v6:
time: 76.1 us; the launch traced here: 75.9 us
  Pallas kernels  74.4 us (98%)
  between operations  1.45 us (2%)
    pallas_call x1, Pallas kernels, local(): pl.pallas_call(kernel, out_shape=(jax.ShapeDtypeStruct((CH, FR, 256), BF1...  72 us
    pallas_call x1, Pallas kernels, local(): pl.pallas_call(results, out_shape=(jax.ShapeDtypeStruct((CH, FR, 256), BF...  2.47 us

profile of v6, /device:TPU:1, one launch (start us, length us, event | category | flops | bytes accessed | tf_op | source)
XLA Modules:
  0.0 75.9 jit_solution(18067145255487766556)
XLA Ops:
  1.3 72.0 %shard_map.129 = (bf16[64,32,256]{2,1,0:T(8,128)(2,1)}, f32[16,2,24,128]{3,2,1,0:T(8,128)}, f32[4,64,256]{2,1,0:T(8,128)}) custom-call(s32[1,4]{1,0:T(1,128)} %block_ids.1, s32[1,4]{1,0:T(1,128)} %weight_ids.1, s32[1]{0:T(128)S(6)} %copy.14.col_start, bf16[4,64,256]{2,1,0:T(8,128)(2,1)} %rest_0_.1, bf16[16,32,256]{2,1,0:T(8,128)(2,1)} %rest_1_.1, ...), custom_call_target="tpu_custom_call" | custom-call | flops 4000000000 | bytes 8000000 | tf_op jit(solution)/shard_map/pallas_call | solution.py:825
  73.3 2.5 %shard_map.130 = (bf16[64,32,256]{2,1,0:T(8,128)(2,1)}, f32[3,3,64,80]{3,2,1,0:T(8,128)}, f32[3,3,64,64]{3,2,1,0:T(8,128)}, f32[4,64,256]{2,1,0:T(8,128)}) custom-call(bf16[64,32,256]{2,1,0:T(8,128)(2,1)} %get-tuple-element.7.fine, f32[16,2,24,128]{3,2,1,0:T(8,128)} %get-tuple-element.8.grads, f32[4,64,256]{2,1,0:T(8,128)} %get-tuple-element.9.block), custom_call_target="tpu_custom_call" | custom-call | flops 270000000 | bytes 4000000 | tf_op jit(solution)/shard_map/pallas_call | solution.py:922
